TPU v7x, 32 devices: a whole 2x2x4 slice. The times are simulated.
32 devices in a mesh: dp: 2 (over core), head: 4 (over y, x), mlp: 4 (over z).
Axes of the slice: x: 2, y: 2, z: 4, core: 2. Of those that a mesh axis runs over, the one named last changes fastest.
Arguments:
- tokens: bfloat16 [2048, 8, 1024], P('head', ('dp', 'mlp')), may hold values from -6 to 6
- first_values: bfloat16 [2048, 8, 1024], P(None, ('dp', 'mlp'), 'head'), may hold values from -10.5 to 10.5
- segment_ids: int32 [2048, 8], P(None, ('dp', 'mlp')), may hold values from 0 to 7, as said below
- positions: int32 [2048, 8], P(None, ('dp', 'mlp')), may hold values from 0 to 2047, as said below
- attn_gain: float32 [1024], replicated, may hold values from 0.5 to 1.5
- w_query: bfloat16 [1024, 1024], P(None, 'head'), may hold values from -0.1875 to 0.1875
- w_key: bfloat16 [1024, 1024], P(None, 'head'), may hold values from -0.1875 to 0.1875
- w_value: bfloat16 [1024, 1024], P(None, 'head'), may hold values from -0.1875 to 0.1875
- w_out: bfloat16 [1024, 1024], P('head'), may hold values from -2 to 2
- mlp_gain: float32 [1024], replicated, may hold values from 0.5 to 1.5
- w_gate: bfloat16 [1024, 2816], P(None, 'mlp'), may hold values from -0.1875 to 0.1875
- w_up: bfloat16 [1024, 2816], P(None, 'mlp'), may hold values from -0.1875 to 0.1875
- w_down: bfloat16 [2816, 1024], P('mlp'), may hold values from -0.109375 to 0.109375
- out_grad: bfloat16 [2048, 8, 1024], P('head', ('dp', 'mlp')), may hold values from -6 to 6
Outputs:
- output: bfloat16 [2048, 8, 1024], P('head', ('dp', 'mlp'))
- input_grad: bfloat16 [2048, 8, 1024], P('head', ('dp', 'mlp'))
- first_values_grad: bfloat16 [2048, 8, 1024], P(None, ('dp', 'mlp'), 'head')
- attn_gain_grad: float32 [1024], replicated
- w_query_grad: float32 [1024, 1024], P(None, 'head')
- w_key_grad: float32 [1024, 1024], P(None, 'head')
- w_value_grad: float32 [1024, 1024], P(None, 'head')
- w_out_grad: float32 [1024, 1024], P('head')
- mlp_gain_grad: float32 [1024], replicated
- w_gate_grad: float32 [1024, 2816], P(None, 'mlp')
- w_up_grad: float32 [1024, 2816], P(None, 'mlp')
- w_down_grad: float32 [2816, 1024], P('mlp')
- value_norms: float32 [2], replicated
Inputs may be any that keep to these rules, and one draw needn't show every extreme that they name: `segment_ids`: along each packed row (dimension 0) the ids start at 0 and rise by at most one from one position to the next; packed row 0 holds a single document, every other packed row exactly 8. `positions`: 0 at a row's start and wherever the segment id changes, else one more than at the previous position.
All inputs are finite; a program needn't handle non-finite values.
Results may differ from a plain program's by a relative error of at most 0.019.
Values may be sent and summed in bfloat16 or wider, within the bound.
No kernel may reach another device: no remote copies, remote signals or barrier semaphores. Data moves between devices by JAX's collectives and lax.ppermute only.
A program may use at most 256 MiB of HBM per device.

v0:
```python
import jax
import jax.numpy as jnp
from jax import lax
from jax.sharding import PartitionSpec as P

HEAD_DIM = 64


epsilon = 1e-06
theta_base = 10000.0
blend_weight = 0.5
masked_score = -1e30


def rms_scale(rows):
    return lax.rsqrt(jnp.mean(rows * rows, axis=-1, keepdims=True) + epsilon)


def norm_back(rows, scale, gain, grad):
    weighted = grad * gain
    row_grad = scale * weighted - rows * scale * scale * scale * jnp.mean(
        weighted * rows, axis=-1, keepdims=True
    )
    gain_grad = jnp.sum(grad * rows * scale, axis=(0, 1))
    return (row_grad, gain_grad)


def rotate(values, places, direction):
    half = values.shape[-1] // 2
    freq = theta_base ** (-jnp.arange(half, dtype=jnp.float32) * 2.0 / values.shape[-1])
    angles = places.astype(jnp.float32)[..., None] * freq
    cosine = jnp.cos(angles)[:, :, None, :]
    sine = direction * jnp.sin(angles)[:, :, None, :]
    first, second = (values[..., :half], values[..., half:])
    return jnp.concatenate(
        [first * cosine - second * sine, second * cosine + first * sine], axis=-1
    )


def by_rows(array, heads):
    return jnp.moveaxis(array.reshape(array.shape[0], array.shape[1], heads, -1), 1, 0)


def block_scores(queries, keys, segments, number, block):
    length = keys.shape[0]
    begin = number * block
    query_block = lax.dynamic_slice_in_dim(queries, begin, block, 0)
    query_index = begin + jnp.arange(block, dtype=jnp.int32)
    key_index = jnp.arange(length, dtype=jnp.int32)
    query_segments = lax.dynamic_slice_in_dim(segments, begin, block, 0)
    allowed = (key_index[None, :] <= query_index[:, None]) & (
        segments[None, :] == query_segments[:, None]
    )
    scores = jnp.einsum(
        "qhd,khd->hqk", query_block, keys, preferred_element_type=jnp.float32
    ) * HEAD_DIM ** (-0.5)
    return (query_block, jnp.where(allowed[None], scores, masked_score))


def attend_forward(queries, keys, values, segments, block):
    length = queries.shape[0]

    def one_block(carry, number):
        query_block, scores = block_scores(queries, keys, segments, number, block)
        top = jnp.max(scores, axis=-1, keepdims=True)
        log_total = top + jnp.log(jnp.sum(jnp.exp(scores - top), axis=-1, keepdims=True))
        weights = jnp.exp(scores - log_total).astype(jnp.bfloat16)
        mixed = jnp.einsum("hqk,khd->qhd", weights, values, preferred_element_type=jnp.float32)
        return (carry, (mixed, log_total))

    _, (mixed, log_total) = lax.scan(one_block, 0, jnp.arange(length // block))
    return (mixed.reshape(length, mixed.shape[2], mixed.shape[3]), log_total)


def attend_backward(queries, keys, values, segments, mixed_grad, log_total, block):
    length = queries.shape[0]
    scale = HEAD_DIM ** (-0.5)

    def one_block(carry, number):
        key_grad, value_grad = carry
        query_block, scores = block_scores(queries, keys, segments, number, block)
        probs = jnp.exp(scores - log_total[number])
        weights = probs.astype(jnp.bfloat16)
        grad_block = lax.dynamic_slice_in_dim(mixed_grad, number * block, block, 0)
        weight_grad = jnp.einsum(
            "qhd,khd->hqk", grad_block, values, preferred_element_type=jnp.float32
        )
        score_grad = (
            probs * (weight_grad - jnp.sum(probs * weight_grad, axis=-1, keepdims=True))
        ).astype(jnp.bfloat16)
        query_grad = (
            jnp.einsum("hqk,khd->qhd", score_grad, keys, preferred_element_type=jnp.float32) * scale
        )
        key_grad = (
            key_grad
            + jnp.einsum(
                "hqk,qhd->khd", score_grad, query_block, preferred_element_type=jnp.float32
            )
            * scale
        )
        value_grad = value_grad + jnp.einsum(
            "hqk,qhd->khd", weights, grad_block, preferred_element_type=jnp.float32
        )
        return ((key_grad, value_grad), query_grad)

    zeros = jnp.zeros(keys.shape, jnp.float32)
    (key_grad, value_grad), query_grad = lax.scan(
        one_block, (zeros, zeros), jnp.arange(length // block)
    )
    return (query_grad.reshape(keys.shape), key_grad, value_grad)


def on_device(
    tokens,
    first_values,
    segment_ids,
    positions,
    attn_gain,
    w_query,
    w_key,
    w_value,
    w_out,
    mlp_gain,
    w_gate,
    w_up,
    w_down,
    out_grad,
):
    width = w_query.shape[1]
    heads_here = width // HEAD_DIM
    length = segment_ids.shape[0]
    rows_here = tokens.shape[1]
    block = min(512, length)
    ff_here = w_gate.shape[1]
    residual = tokens.astype(jnp.float32)
    attn_scale = rms_scale(residual)
    attn_input = (residual * attn_scale * attn_gain).astype(jnp.bfloat16)
    w_project = jnp.concatenate([w_query, w_key, w_value], axis=1)
    piece = lax.all_gather(attn_input, "head", axis=0, tiled=True)
    count = piece.shape[0]
    joined = jnp.einsum("lrd,dh->lrh", piece, w_project, preferred_element_type=jnp.float32)
    query_part = joined[..., :width].reshape(count, rows_here, heads_here, HEAD_DIM)
    key_part = joined[..., width : 2 * width].reshape(count, rows_here, heads_here, HEAD_DIM)
    queries = (
        rotate(query_part, positions, 1.0).reshape(count, rows_here, width).astype(jnp.bfloat16)
    )
    keys = rotate(key_part, positions, 1.0).reshape(count, rows_here, width).astype(jnp.bfloat16)
    gathered, queries, keys, value_proj = (piece, queries, keys, joined[..., 2 * width :])
    firsts = first_values.astype(jnp.float32)
    blended = blend_weight * value_proj + (1.0 - blend_weight) * firsts
    blended_low = blended.astype(jnp.bfloat16)
    first_heads = firsts.reshape(length, rows_here, heads_here, HEAD_DIM)
    blend_heads = blended.reshape(length, rows_here, heads_here, HEAD_DIM)
    norm_local = jnp.stack(
        [
            jnp.sum(jnp.sqrt(jnp.sum(first_heads * first_heads, axis=-1))),
            jnp.sum(jnp.sqrt(jnp.sum(blend_heads * blend_heads, axis=-1))),
        ]
    )
    segment_rows = jnp.transpose(segment_ids, (1, 0))
    query_rows = by_rows(queries, heads_here)
    key_rows = by_rows(keys, heads_here)
    value_rows = by_rows(blended_low, heads_here)

    def forward_row(item):
        return attend_forward(item[0], item[1], item[2], item[3], block)

    mixed, log_total = lax.map(forward_row, (query_rows, key_rows, value_rows, segment_rows))
    attn_mixed = jnp.moveaxis(mixed, 0, 1).reshape(length, rows_here, width).astype(jnp.bfloat16)
    part = attn_mixed
    attn_branch = lax.psum_scatter(
        jnp.einsum("lrh,hd->lrd", part, w_out, preferred_element_type=jnp.float32),
        "head",
        scatter_dimension=0,
        tiled=True,
    )
    hidden_state = residual + attn_branch
    mlp_scale = rms_scale(hidden_state)
    mlp_input = (hidden_state * mlp_scale * mlp_gain).astype(jnp.bfloat16)
    w_gate_up = jnp.concatenate([w_gate, w_up], axis=1)
    piece = lax.all_gather(mlp_input, "mlp", axis=1, tiled=True)
    joined = jnp.einsum("lrd,df->lrf", piece, w_gate_up, preferred_element_type=jnp.float32)
    gate = joined[..., :ff_here]
    up = joined[..., ff_here:]
    expand_hidden = (jax.nn.silu(gate) * up).astype(jnp.bfloat16)
    mlp_gathered = piece
    down_terms = jnp.einsum(
        "lrf,fd->lrd", expand_hidden, w_down, preferred_element_type=jnp.float32
    )
    mlp_branch = lax.psum_scatter(
        down_terms.astype(jnp.bfloat16), "mlp", scatter_dimension=1, tiled=True
    ).astype(jnp.float32)
    output = (hidden_state + mlp_branch).astype(jnp.bfloat16)
    piece = lax.all_gather(out_grad, "mlp", axis=1, tiled=True)
    down_sum = jnp.einsum("lrf,lrd->fd", expand_hidden, piece, preferred_element_type=jnp.float32)
    part_grad = jnp.einsum("lrd,fd->lrf", piece, w_down, preferred_element_type=jnp.float32)
    hidden_grad = part_grad
    gate, up = (gate, up)
    sigma = jax.nn.sigmoid(gate)
    gate_grad = (hidden_grad * up * sigma * (1.0 + gate * (1.0 - sigma))).astype(jnp.bfloat16)
    up_grad = (hidden_grad * gate * sigma).astype(jnp.bfloat16)
    gate_up_grad = jnp.concatenate([gate_grad, up_grad], axis=-1)
    gate_up_wgrad = jnp.einsum(
        "lrd,lrf->df", mlp_gathered, gate_up_grad, preferred_element_type=jnp.float32
    )
    input_terms = jnp.einsum(
        "lrf,df->lrd", gate_up_grad, w_gate_up, preferred_element_type=jnp.float32
    )
    mlp_normed_grad = lax.psum_scatter(
        input_terms.astype(jnp.bfloat16), "mlp", scatter_dimension=1, tiled=True
    ).astype(jnp.float32)
    state_norm_grad, mlp_gain_grad = norm_back(hidden_state, mlp_scale, mlp_gain, mlp_normed_grad)
    state_grad = out_grad.astype(jnp.float32) + state_norm_grad
    state_grad_low = state_grad.astype(jnp.bfloat16)
    piece = lax.all_gather(state_grad_low, "head", axis=0, tiled=True)
    out_sum = jnp.einsum("lrh,lrd->hd", attn_mixed, piece, preferred_element_type=jnp.float32)
    part_grad = jnp.einsum("lrd,hd->lrh", piece, w_out, preferred_element_type=jnp.float32)
    out_wgrad = out_sum
    mixed_grad_low = part_grad.astype(jnp.bfloat16)
    mixed_grad_rows = by_rows(mixed_grad_low, heads_here)

    def backward_row(item):
        return attend_backward(item[0], item[1], item[2], item[3], item[4], item[5], block)

    query_grad, key_grad, blend_grad = lax.map(
        backward_row, (query_rows, key_rows, value_rows, segment_rows, mixed_grad_rows, log_total)
    )
    query_grad = jnp.moveaxis(query_grad, 0, 1)
    key_grad = jnp.moveaxis(key_grad, 0, 1)
    blend_low = (
        jnp.moveaxis(blend_grad, 0, 1).reshape(length, rows_here, width).astype(jnp.bfloat16)
    )
    query_pre = (
        rotate(query_grad, positions, -1.0).reshape(length, rows_here, width).astype(jnp.bfloat16)
    )
    key_pre = (
        rotate(key_grad, positions, -1.0).reshape(length, rows_here, width).astype(jnp.bfloat16)
    )
    value_pre = (blend_weight * blend_low.astype(jnp.float32)).astype(jnp.bfloat16)
    first_values_grad = ((1.0 - blend_weight) * blend_low.astype(jnp.float32)).astype(jnp.bfloat16)
    proj_grad = jnp.concatenate([query_pre, key_pre, value_pre], axis=-1)
    proj_wgrad = jnp.einsum("lrd,lrh->dh", gathered, proj_grad, preferred_element_type=jnp.float32)
    part = proj_grad
    attn_normed_grad = lax.psum_scatter(
        jnp.einsum("lrh,dh->lrd", part, w_project, preferred_element_type=jnp.float32).astype(
            jnp.bfloat16
        ),
        "head",
        scatter_dimension=0,
        tiled=True,
    ).astype(jnp.float32)
    input_norm_grad, attn_gain_grad = norm_back(residual, attn_scale, attn_gain, attn_normed_grad)
    input_grad = (state_grad + input_norm_grad).astype(jnp.bfloat16)
    query_wgrad, key_wgrad, value_wgrad, out_wgrad = (
        lax.psum(proj_wgrad[:, :width].astype(jnp.bfloat16), ("dp", "mlp")).astype(jnp.float32),
        lax.psum(proj_wgrad[:, width : 2 * width].astype(jnp.bfloat16), ("dp", "mlp")).astype(
            jnp.float32
        ),
        lax.psum(proj_wgrad[:, 2 * width :].astype(jnp.bfloat16), ("dp", "mlp")).astype(
            jnp.float32
        ),
        lax.psum(out_wgrad.astype(jnp.bfloat16), ("dp", "mlp")).astype(jnp.float32),
    )
    gate_wgrad, up_wgrad, down_wgrad = (
        lax.psum(gate_up_wgrad[:, :ff_here].astype(jnp.bfloat16), ("dp", "head")).astype(
            jnp.float32
        ),
        lax.psum(gate_up_wgrad[:, ff_here:].astype(jnp.bfloat16), ("dp", "head")).astype(
            jnp.float32
        ),
        lax.psum(down_sum.astype(jnp.bfloat16), ("dp", "head")).astype(jnp.float32),
    )
    attn_gain_total, mlp_gain_total, norm_total = lax.psum(
        (attn_gain_grad, mlp_gain_grad, norm_local), ("dp", "head", "mlp")
    )
    count_all = (
        length
        * rows_here
        * heads_here
        * lax.axis_size("dp")
        * lax.axis_size("head")
        * lax.axis_size("mlp")
    )
    value_norms = norm_total / count_all
    return (
        output,
        input_grad,
        first_values_grad,
        attn_gain_total,
        query_wgrad,
        key_wgrad,
        value_wgrad,
        out_wgrad,
        mlp_gain_total,
        gate_wgrad,
        up_wgrad,
        down_wgrad,
        value_norms,
    )


def solution(mesh):
    placed = (
        P("head", ("dp", "mlp"), None),
        P(None, ("dp", "mlp"), "head"),
        P(None, ("dp", "mlp")),
        P(None, ("dp", "mlp")),
        P(),
        P(None, "head"),
        P(None, "head"),
        P(None, "head"),
        P("head", None),
        P(),
        P(None, "mlp"),
        P(None, "mlp"),
        P("mlp", None),
        P("head", ("dp", "mlp"), None),
    )
    return jax.shard_map(
        on_device,
        mesh=mesh,
        in_specs=placed,
        out_specs=(
            P("head", ("dp", "mlp"), None),
            P("head", ("dp", "mlp"), None),
            P(None, ("dp", "mlp"), "head"),
            P(),
            P(None, "head"),
            P(None, "head"),
            P(None, "head"),
            P("head", None),
            P(),
            P(None, "mlp"),
            P(None, "mlp"),
            P("mlp", None),
            P(),
        ),
        check_vma=False,
    )
```

profile of v0, /device:TPU:0, one launch (start us, length us, event | category | flops | bytes accessed | tf_op | source)
XLA Modules:
  0.0 1060.9 jit_solution(17914866796289467341)
XLA Ops:
  19.0 48.6 %all-gather.5.cloned.1.call-done = bf16[2048,1,1024]{2,0,1:T(8,128)(2,1)} async-done(((bf16[512,1,1024]{2,0,1:T(8,128)(2,1)}), bf16[2048,1,1024]{2,0,1:T(8,128)(2,1)}) %all-gather.5.cloned.1.call-update) | async-done | bytes 4194320 | tf_op jit(solution)/shard_map/all_gather | solution.py:139
  67.6 5.8 fusion.45
  78.5 68.2 %while.47 = (s32[]{:T(128)}, bf16[4,512,4,64]{1,3,2,0:T(8,128)(2,1)}, f32[4,4,512,1]{2,1,3,0:T(4,128)}, s32[4]{0:T(128)S(1)}, s32[2048]{0:T(1024)S(1)}, /*index=...) while((s32[]{:T(128)}, ...), condition=%wide.region_4.0_spmd, body=%wide.region_1.4_spmd.sunk | while | flops 1123023360 | bytes 65882372 | solution.py:71
  89.2 5.5 fusion.136
  106.2 5.5 fusion.136
  123.2 5.5 fusion.136
  140.2 5.5 fusion.136
  150.4 4.6 convolution_bitcast_fusion
  155.0 86.5 %reduce-scatter.5.cloned.1.call-done = f32[512,1,1024]{2,0,1:T(8,128)} async-done(((f32[2048,1,1024]{2,0,1:T(8,128)}), f32[512,1,1024]{2,0,1:T(8,128)}) %reduce-scatter.5.cloned.1.call-update) | async-done | bytes 2097168 | tf_op jit(solution)/shard_map/reduce_scatter | solution.py:171
  253.5 75.0 %all-gather.7.cloned.1.call-done = bf16[512,4,1024]{2,0,1:T(8,128)(2,1)} async-done(((bf16[512,1,1024]{2,0,1:T(8,128)(2,1)}), bf16[512,4,1024]{2,0,1:T(8,128)(2,1)}) %all-gather.7.cloned.1.call-update) | async-done | bytes 4194320 | tf_op jit(solution)/shard_map/all_gather | solution.py:181
  328.5 13.2 %fusion.74 = f32[512,4,1408]{0,2,1:T(8,128)} fusion(bf16[512,4,1024]{2,0,1:T(8,128)(2,1)} %all-gather.7.cloned.1.call-done, bf16[1024,704]{1,0:T(8,128)(2,1)} %copy.69, bf16[1024,704]{1,0:T(8,128)(2,1)} %copy.68), kind=kOutput, calls=%fused_computation.106 | convolution fusion | flops 5911347200 | bytes 18612224 | tf_op jit(solution)/shard_map/lrd,df->lrf/dot_general | solution.py:182
  341.7 67.6 %all-gather.9.cloned.1.call-done = bf16[512,4,1024]{2,0,1:T(8,128)(2,1)} async-done(((bf16[512,1,1024]{2,0,1:T(8,128)(2,1)}), bf16[512,4,1024]{2,0,1:T(8,128)(2,1)}) %all-gather.9.cloned.1.call-update) | async-done | bytes 4194320 | tf_op jit(solution)/shard_map/all_gather | solution.py:194
  409.3 10.6 multiply_convert_fusion.2
  422.4 9.5 fusion.49
  432.4 75.0 %reduce-scatter.9.cloned.1.call-done = bf16[512,1,1024]{2,0,1:T(8,128)(2,1)} async-done(((bf16[512,4,1024]{2,0,1:T(8,128)(2,1)}), bf16[512,1,1024]{2,0,1:T(8,128)(2,1)}) %reduce-scatter.9.cloned.1.call-update) | async-done | bytes 1048592 | tf_op jit(solution)/shard_map/reduce_scatter | solution.py:209
  514.7 10.4 bitcast_convert_fusion
  532.8 35.1 %all-gather.11.cloned.1.call-done = bf16[2048,1,1024]{2,0,1:T(8,128)(2,1)} async-done(((bf16[512,1,1024]{2,0,1:T(8,128)(2,1)}), bf16[2048,1,1024]{2,0,1:T(8,128)(2,1)}) %all-gather.11.cloned.1.call-update) | async-done | bytes 4194320 | tf_op jit(solution)/shard_map/all_gather | solution.py:215
  568.0 4.4 fusion.50
  572.4 260.4 %while.48 = (s32[]{:T(128)}, f32[2048,4,64]{0,2,1:T(8,128)}, f32[2048,4,64]{0,2,1:T(8,128)}, f32[4,512,4,64]{1,0,3,2:T(4,128)}, s32[4]{0:T(128)S(1)}, /*index=5*...) while((s32[]{:T(128)}, f32[2048,4,64]{0,2,1:T(8,128)}, ...), condition=%wide.region_12.13_spmd.clone, body=%wide.region_10.12_spmd.clone.sunk | while | flops 2753165824 | bytes 212412720 | solution.py:107
  580.6 5.8 copy-done.1
  586.5 7.2 fusion.149
  593.6 13.0 %multiply_reduce_fusion.3 = (f32[4,512]{1,0:T(4,128)S(1)}, f32[4,512,2048]{2,1,0:T(8,128)}) fusion(f32[4,512,2048]{2,1,0:T(8,128)} %copy-done.1, f32[4,512]{1,0:T(4,128)S(1)} %dynamic-slice_bitcast_fusion.2, pred[512,2048]{1,0:T(8,128)(4,1)S(1)} %fusion.147, bf16[2048,4,64]{0,2,1:T(8,128)(2,1)} %get-tuple-element.557, ...), kind=kOutput, calls=%fused_computation.19.clone.1 | convolution fusion | flops 557840384 | bytes 35930116 | tf_op jit(solution)/shard_map/while/body/eval_jaxpr/while/body/eval_jaxpr/qhd,khd->hqk/dot_general | solution.py:85
  606.6 12.3 %multiply_convert_fusion.7 = bf16[4,512,2048]{2,1,0:T(8,128)(2,1)S(1)} fusion(f32[4,512,2048]{2,1,0:T(8,128)} %get-tuple-element.477, f32[4,512,2048]{2,1,0:T(8,128)} %copy-done.1, f32[4,512]{1,0:T(4,128)S(1)} %get-tuple-element.478, f32[4,512]{1,0:T(4,128)S(1)} %dynamic-slice_bitcast_fusion.2, pred[512,2048]{1,0:T(8,128)(4,1)S(1)} %fusion.147), kind=kLoop, calls=%fused_computation.18.clone.1 | loop fusion | flops 25165824 | bytes 43008000 | tf_op jit(solution)/shard_map/while/body/eval_jaxpr/while/body/eval_jaxpr/convert_element_type | solution.py:90
  626.0 11.1 %dynamic_update_slice.31 = f32[4,512,4,64]{1,0,3,2:T(4,128)} dynamic-update-slice(f32[4,512,4,64]{1,0,3,2:T(4,128)} %get-tuple-element.534, f32[1,512,4,64]{1,0,3,2:T(1,128)S(1)} %copy.97, s32[]{:T(128)S(6)} %copy.116, s32[]{:T(128)} %constant.102.clone.1..sunk.1, s32[]{:T(128)} %constant.102.clone.1..sunk.1, s32[]{:T(128)} %constant.102.clone.1..sunk.1) | dynamic-update-slice | bytes 1048580 | tf_op jit(solution)/shard_map/while/body/eval_jaxpr/while/body/jit(dynamic_update_index_in_dim)/dynamic_update_slice | solution.py:71
  645.1 5.9 copy-done.1
  651.0 7.6 fusion.149
  658.6 12.8 %multiply_reduce_fusion.3 = (f32[4,512]{1,0:T(4,128)S(1)}, f32[4,512,2048]{2,1,0:T(8,128)}) fusion(f32[4,512,2048]{2,1,0:T(8,128)} %copy-done.1, f32[4,512]{1,0:T(4,128)S(1)} %dynamic-slice_bitcast_fusion.2, pred[512,2048]{1,0:T(8,128)(4,1)S(1)} %fusion.147, bf16[2048,4,64]{0,2,1:T(8,128)(2,1)} %get-tuple-element.557, ...), kind=kOutput, calls=%fused_computation.19.clone.1 | convolution fusion | flops 557840384 | bytes 35930116 | tf_op jit(solution)/shard_map/while/body/eval_jaxpr/while/body/eval_jaxpr/qhd,khd->hqk/dot_general | solution.py:85
  671.4 12.1 %multiply_convert_fusion.7 = bf16[4,512,2048]{2,1,0:T(8,128)(2,1)S(1)} fusion(f32[4,512,2048]{2,1,0:T(8,128)} %get-tuple-element.477, f32[4,512,2048]{2,1,0:T(8,128)} %copy-done.1, f32[4,512]{1,0:T(4,128)S(1)} %get-tuple-element.478, f32[4,512]{1,0:T(4,128)S(1)} %dynamic-slice_bitcast_fusion.2, pred[512,2048]{1,0:T(8,128)(4,1)S(1)} %fusion.147), kind=kLoop, calls=%fused_computation.18.clone.1 | loop fusion | flops 25165824 | bytes 43008000 | tf_op jit(solution)/shard_map/while/body/eval_jaxpr/while/body/eval_jaxpr/convert_element_type | solution.py:90
  686.1 4.7 fusion.148
  691.3 11.1 %dynamic_update_slice.31 = f32[4,512,4,64]{1,0,3,2:T(4,128)} dynamic-update-slice(f32[4,512,4,64]{1,0,3,2:T(4,128)} %get-tuple-element.534, f32[1,512,4,64]{1,0,3,2:T(1,128)S(1)} %copy.97, s32[]{:T(128)S(6)} %copy.116, s32[]{:T(128)} %constant.102.clone.1..sunk.1, s32[]{:T(128)} %constant.102.clone.1..sunk.1, s32[]{:T(128)} %constant.102.clone.1..sunk.1) | dynamic-update-slice | bytes 1048580 | tf_op jit(solution)/shard_map/while/body/eval_jaxpr/while/body/jit(dynamic_update_index_in_dim)/dynamic_update_slice | solution.py:71
  710.4 5.7 copy-done.1
  716.1 7.5 fusion.149
  723.7 12.8 %multiply_reduce_fusion.3 = (f32[4,512]{1,0:T(4,128)S(1)}, f32[4,512,2048]{2,1,0:T(8,128)}) fusion(f32[4,512,2048]{2,1,0:T(8,128)} %copy-done.1, f32[4,512]{1,0:T(4,128)S(1)} %dynamic-slice_bitcast_fusion.2, pred[512,2048]{1,0:T(8,128)(4,1)S(1)} %fusion.147, bf16[2048,4,64]{0,2,1:T(8,128)(2,1)} %get-tuple-element.557, ...), kind=kOutput, calls=%fused_computation.19.clone.1 | convolution fusion | flops 557840384 | bytes 35930116 | tf_op jit(solution)/shard_map/while/body/eval_jaxpr/while/body/eval_jaxpr/qhd,khd->hqk/dot_general | solution.py:85
  736.5 12.1 %multiply_convert_fusion.7 = bf16[4,512,2048]{2,1,0:T(8,128)(2,1)S(1)} fusion(f32[4,512,2048]{2,1,0:T(8,128)} %get-tuple-element.477, f32[4,512,2048]{2,1,0:T(8,128)} %copy-done.1, f32[4,512]{1,0:T(4,128)S(1)} %get-tuple-element.478, f32[4,512]{1,0:T(4,128)S(1)} %dynamic-slice_bitcast_fusion.2, pred[512,2048]{1,0:T(8,128)(4,1)S(1)} %fusion.147), kind=kLoop, calls=%fused_computation.18.clone.1 | loop fusion | flops 25165824 | bytes 43008000 | tf_op jit(solution)/shard_map/while/body/eval_jaxpr/while/body/eval_jaxpr/convert_element_type | solution.py:90
  751.2 4.7 fusion.148
  756.4 11.1 %dynamic_update_slice.31 = f32[4,512,4,64]{1,0,3,2:T(4,128)} dynamic-update-slice(f32[4,512,4,64]{1,0,3,2:T(4,128)} %get-tuple-element.534, f32[1,512,4,64]{1,0,3,2:T(1,128)S(1)} %copy.97, s32[]{:T(128)S(6)} %copy.116, s32[]{:T(128)} %constant.102.clone.1..sunk.1, s32[]{:T(128)} %constant.102.clone.1..sunk.1, s32[]{:T(128)} %constant.102.clone.1..sunk.1) | dynamic-update-slice | bytes 1048580 | tf_op jit(solution)/shard_map/while/body/eval_jaxpr/while/body/jit(dynamic_update_index_in_dim)/dynamic_update_slice | solution.py:71
  775.5 5.7 copy-done.1
  781.2 7.6 fusion.149
  788.8 12.8 %multiply_reduce_fusion.3 = (f32[4,512]{1,0:T(4,128)S(1)}, f32[4,512,2048]{2,1,0:T(8,128)}) fusion(f32[4,512,2048]{2,1,0:T(8,128)} %copy-done.1, f32[4,512]{1,0:T(4,128)S(1)} %dynamic-slice_bitcast_fusion.2, pred[512,2048]{1,0:T(8,128)(4,1)S(1)} %fusion.147, bf16[2048,4,64]{0,2,1:T(8,128)(2,1)} %get-tuple-element.557, ...), kind=kOutput, calls=%fused_computation.19.clone.1 | convolution fusion | flops 557840384 | bytes 35930116 | tf_op jit(solution)/shard_map/while/body/eval_jaxpr/while/body/eval_jaxpr/qhd,khd->hqk/dot_general | solution.py:85
  801.6 12.1 %multiply_convert_fusion.7 = bf16[4,512,2048]{2,1,0:T(8,128)(2,1)S(1)} fusion(f32[4,512,2048]{2,1,0:T(8,128)} %get-tuple-element.477, f32[4,512,2048]{2,1,0:T(8,128)} %copy-done.1, f32[4,512]{1,0:T(4,128)S(1)} %get-tuple-element.478, f32[4,512]{1,0:T(4,128)S(1)} %dynamic-slice_bitcast_fusion.2, pred[512,2048]{1,0:T(8,128)(4,1)S(1)} %fusion.147), kind=kLoop, calls=%fused_computation.18.clone.1 | loop fusion | flops 25165824 | bytes 43008000 | tf_op jit(solution)/shard_map/while/body/eval_jaxpr/while/body/eval_jaxpr/convert_element_type | solution.py:90
  816.3 4.7 fusion.148
  821.5 11.1 %dynamic_update_slice.31 = f32[4,512,4,64]{1,0,3,2:T(4,128)} dynamic-update-slice(f32[4,512,4,64]{1,0,3,2:T(4,128)} %get-tuple-element.534, f32[1,512,4,64]{1,0,3,2:T(1,128)S(1)} %copy.97, s32[]{:T(128)S(6)} %copy.116, s32[]{:T(128)} %constant.102.clone.1..sunk.1, s32[]{:T(128)} %constant.102.clone.1..sunk.1, s32[]{:T(128)} %constant.102.clone.1..sunk.1) | dynamic-update-slice | bytes 1048580 | tf_op jit(solution)/shard_map/while/body/eval_jaxpr/while/body/jit(dynamic_update_index_in_dim)/dynamic_update_slice | solution.py:71
  848.8 7.2 convert_bitcast_fusion
  856.0 7.2 convolution_convert_fusion
  881.1 33.1 %all-reduce.6.cloned.1.call-done = (bf16[1024,256]{1,0:T(8,128)(2,1)}, bf16[1024,256]{1,0:T(8,128)(2,1)}, bf16[1024,256]{1,0:T(8,128)(2,1)}, bf16[256,1024]{1,0:T(8,128)(2,1)}) async-done(((bf16[1024,256]{1,0:T(8,128)(2,1)}, bf16[1024,256]{1,0:T(8,128)(2,1)}, bf16[1024,256]{1,0:T(8,128)(2,1)}, bf16[256,1024]{1,0:T(8,128)(2,1)}), (bf16[1024,256]{1,0:T(8,128)(2,1)}, bf16[1024,256]{1,0:T(8,128)(2,1)}, ...) | async-done | bytes 2097168 | tf_op jit(solution)/shard_map/psum | solution.py:255
  920.7 48.6 %reduce-scatter.11.cloned.1.call-done = bf16[512,1,1024]{2,0,1:T(8,128)(2,1)} async-done(((bf16[2048,1,1024]{2,0,1:T(8,128)(2,1)}), bf16[512,1,1024]{2,0,1:T(8,128)(2,1)}) %reduce-scatter.11.cloned.1.call-update) | async-done | bytes 1048592 | tf_op jit(solution)/shard_map/reduce_scatter | solution.py:244
  972.0 42.0 %all-reduce = (f32[1024]{0:T(1024)}, f32[1024]{0:T(1024)}, f32[2]{0:T(128)}) all-reduce(f32[1024]{0:T(1024)} %get-tuple-element.261, f32[1024]{0:T(1024)} %get-tuple-element.259, f32[2]{0:T(128)} %pad_maximum_fusion.7), channel_id=1, replica_groups=mesh['dp'=2,'head'=4,'mlp'=4] {'dp','head','mlp'}, use_global_device_ids=true, to_apply=%region_16.17 | all-reduce | flops 2050 | bytes 16400 | tf_op jit(solution)/shard_map/psum | solution.py:273
  1016.5 32.9 %reduce-scatter.7.cloned.1.call-done = bf16[512,1,1024]{2,0,1:T(8,128)(2,1)} async-done(((bf16[512,4,1024]{2,0,1:T(8,128)(2,1)}), bf16[512,1,1024]{2,0,1:T(8,128)(2,1)}) %reduce-scatter.7.cloned.1.call-update) | async-done | bytes 1048592 | tf_op jit(solution)/shard_map/reduce_scatter | solution.py:190
  (239 shorter events, 182.9 us)
Async XLA Ops:
  7.2 402.2 %copy-start = (bf16[704,1024]{1,0:T(8,128)(2,1)S(1)}, bf16[704,1024]{1,0:T(8,128)(2,1)}, u32[]{:S(2)}) copy-start(bf16[704,1024]{1,0:T(8,128)(2,1)} %param.30) | copy-start | bytes 4325380
  7.2 4.9 copy-start.36
  7.2 4.9 copy-start.19
  7.2 60.4 %all-gather.5.cloned.1.call-start = ((), (), s32[]{:S(2)}) async-start(), calls=%async_computation.4 | async-start | bytes 5242880 | tf_op jit(solution)/shard_map/all_gather | solution.py:139
  12.0 229.5 %reduce-scatter.5.cloned.1.call-start = ((), (), s32[]{:S(2)}) async-start(), calls=%async_computation.5 | async-start | bytes 10485760 | tf_op jit(solution)/shard_map/reduce_scatter | solution.py:171
  19.0 58.1 %copy-start.13 = (f32[2048,32]{0,1:T(8,128)}, f32[2048,32]{0,1:T(8,128)S(1)}, u32[]{:S(2)}) copy-start(f32[2048,32]{0,1:T(8,128)S(1)} %get-tuple-element.348) | copy-start | bytes 786436
  84.2 5.0 copy-start.20
  101.2 5.0 copy-start.20
  118.2 5.0 copy-start.20
  135.2 5.0 copy-start.20
  146.7 8.3 copy-start.4
  146.7 3.7 copy-start.23
  154.9 86.6 %copy-start.2 = (bf16[512,1,1024]{2,0,1:T(8,128)(2,1)S(1)}, bf16[512,1,1024]{2,0,1:T(8,128)(2,1)}, u32[]{:S(2)}) copy-start(bf16[512,1,1024]{2,0,1:T(8,128)(2,1)} %param.18) | copy-start | bytes 3145732
  155.0 89.8 %copy-start.28 = (f32[1024]{0:T(1024)S(1)}, f32[1024]{0:T(1024)}, u32[]{:S(2)}) copy-start(f32[1024]{0:T(1024)} %param.27) | copy-start | bytes 12292
  155.0 173.5 %all-gather.7.cloned.1.call-start = ((), (), s32[]{:S(2)}) async-start(), calls=%async_computation.6 | async-start | bytes 5242880 | tf_op jit(solution)/shard_map/all_gather | solution.py:181
  244.8 265.9 %copy-start.30 = (f32[512]{0:T(512)}, f32[512]{0:T(512)S(1)}, u32[]{:S(2)}) copy-start(f32[512]{0:T(512)S(1)} %add_rsqrt_fusion) | copy-start | bytes 6148
  247.6 161.7 %all-gather.9.cloned.1.call-start = ((), (), s32[]{:S(2)}) async-start(), calls=%async_computation.8 | async-start | bytes 5242880 | tf_op jit(solution)/shard_map/all_gather | solution.py:194
  248.2 259.2 %reduce-scatter.9.cloned.1.call-start = ((), (), s32[]{:S(2)}) async-start(), calls=%async_computation.9 | async-start | bytes 5242880 | tf_op jit(solution)/shard_map/reduce_scatter | solution.py:209
  409.3 13.1 %copy-start.16 = (bf16[1024,704]{1,0:T(8,128)(2,1)S(1)}, bf16[1024,704]{1,0:T(8,128)(2,1)}, u32[]{:S(2)}) copy-start(bf16[1024,704]{1,0:T(8,128)(2,1)} %copy.68) | copy-start | bytes 4325380
  409.3 13.1 %copy-start.17 = (bf16[1024,704]{1,0:T(8,128)(2,1)S(1)}, bf16[1024,704]{1,0:T(8,128)(2,1)}, u32[]{:S(2)}) copy-start(bf16[1024,704]{1,0:T(8,128)(2,1)} %copy.69) | copy-start | bytes 4325380
  431.9 79.3 %copy-start.5 = (bf16[512,1,1024]{2,0,1:T(8,128)(2,1)S(1)}, bf16[512,1,1024]{2,0,1:T(8,128)(2,1)}, u32[]{:S(2)}) copy-start(bf16[512,1,1024]{2,0,1:T(8,128)(2,1)} %param.31) | copy-start | bytes 3145732
  431.9 136.0 %all-gather.11.cloned.1.call-start = ((), (), s32[]{:S(2)}) async-start(), calls=%async_computation.10 | async-start | bytes 5242880 | tf_op jit(solution)/shard_map/all_gather | solution.py:215
  507.4 3.9 copy-start.7
  514.6 356.7 %all-reduce.8.cloned.1.call-start = ((), (), s32[]{:S(2)}) async-start(), calls=%async_computation.13 | async-start | bytes 9175040 | tf_op jit(solution)/shard_map/psum | solution.py:265
  514.7 12.8 %copy-start.40 = (bf16[512,4,704]{0,2,1:T(8,128)(2,1)S(1)}, bf16[512,4,704]{0,2,1:T(8,128)(2,1)}, u32[]{:S(2)}) copy-start(bf16[512,4,704]{0,2,1:T(8,128)(2,1)} %get-tuple-element.321) | copy-start | bytes 8650756
  525.1 3.3 copy-start.39
  532.8 35.2 %copy-start.24 = (bf16[256,1024]{1,0:T(8,128)(2,1)S(1)}, bf16[256,1024]{1,0:T(8,128)(2,1)}, u32[]{:S(2)}) copy-start(bf16[256,1024]{1,0:T(8,128)(2,1)} %param.26) | copy-start | bytes 1572868
  532.8 381.4 %all-reduce.6.cloned.1.call-start = ((), (), s32[]{:S(2)}) async-start(), calls=%async_computation.12 | async-start | bytes 4194304 | tf_op jit(solution)/shard_map/psum | solution.py:255
  580.6 5.9 copy-start.1
  645.1 5.9 copy-start.1
  710.4 5.8 copy-start.1
  775.5 5.8 copy-start.1
  837.9 3.3 copy-start.37
  838.1 6.7 copy-start.22
  840.0 8.8 copy-start.11
  841.2 4.7 copy-start.38
  848.7 120.6 %reduce-scatter.11.cloned.1.call-start = ((), (), s32[]{:S(2)}) async-start(), calls=%async_computation.11 | async-start | bytes 5242880 | tf_op jit(solution)/shard_map/reduce_scatter | solution.py:244
  856.0 193.4 %reduce-scatter.7.cloned.1.call-start = ((), (), s32[]{:S(2)}) async-start(), calls=%async_computation.7 | async-start | bytes 5242880 | tf_op jit(solution)/shard_map/reduce_scatter | solution.py:190
  871.3 3.1 copy-start.15
  876.4 3.4 copy-start.12
  914.2 4.3 copy-start.26
  914.2 5.4 copy-start.25
  914.2 55.1 %copy-start.3 = (bf16[512,1,1024]{2,0,1:T(8,128)(2,1)S(1)}, bf16[512,1,1024]{2,0,1:T(8,128)(2,1)}, u32[]{:S(2)}) copy-start(bf16[512,1,1024]{2,0,1:T(8,128)(2,1)} %param.18) | copy-start | bytes 3145732
  914.2 55.1 %copy-start.32 = (f32[1024]{0:T(1024)S(1)}, f32[1024]{0:T(1024)}, u32[]{:S(2)}) copy-start(f32[1024]{0:T(1024)} %param.22) | copy-start | bytes 12292
  914.2 55.1 %copy-start.34 = (f32[512]{0:T(512)S(1)}, f32[512]{0:T(512)}, u32[]{:S(2)}) copy-start(f32[512]{0:T(512)} %copy-done.33) | copy-start | bytes 6148
  918.5 130.9 %copy-start.6 = (bf16[512,1,1024]{2,0,1:T(8,128)(2,1)S(1)}, bf16[512,1,1024]{2,0,1:T(8,128)(2,1)}, u32[]{:S(2)}) copy-start(bf16[512,1,1024]{2,0,1:T(8,128)(2,1)} %param.31) | copy-start | bytes 3145732
  918.5 130.9 %copy-start.29 = (f32[1024]{0:T(1024)S(1)}, f32[1024]{0:T(1024)}, u32[]{:S(2)}) copy-start(f32[1024]{0:T(1024)} %param.27) | copy-start | bytes 12292
  918.5 130.9 %copy-start.31 = (f32[512]{0:T(512)S(1)}, f32[512]{0:T(512)}, u32[]{:S(2)}) copy-start(f32[512]{0:T(512)} %copy-done.30) | copy-start | bytes 6148
  (14 other events, 18.4 us)
Sparse Core Ops, SparseCore 0:
  12.2 55.3 all-gather.4
  155.1 86.4 reduce-scatter.4
  247.7 80.7 all-gather.6
  330.0 79.2 all-gather.8
  432.0 75.2 reduce-scatter.8
  514.7 53.1 all-gather.10
  572.2 85.7 all-reduce.7
  848.8 65.3 all-reduce.5
  917.2 52.1 reduce-scatter.10
  971.6 77.7 reduce-scatter.6
where the time goes:
time: 1070 us; the launch traced here: 1060 us
  waiting for transfers between devices  503 us (47%)
  matrix products  241 us (23%)
  other arithmetic  130 us (12%)
  local copies, waits for them, and re-layouts  117 us (11%)
  blocking collectives  42 us (4%)
  between operations  14.8 us (1%)
  loops' own time  12.4 us (1%)
    reduce_scatter x1, waiting for transfers between devices, on_device(): lax.psum_scatter(jnp.einsum('lrh,hd->lrd', part, w_out, preferred_element...  86.5 us
    reduce_scatter x1, waiting for transfers between devices, on_device(): lax.psum_scatter(input_terms.astype(jnp.bfloat16), 'mlp', scatter_dimensi...  75 us
    all_gather x1, waiting for transfers between devices, on_device(): piece = lax.all_gather(mlp_input, 'mlp', axis=1, tiled=True)  75 us
    all_gather x1, waiting for transfers between devices, on_device(): piece = lax.all_gather(out_grad, 'mlp', axis=1, tiled=True)  67.6 us
    dot_general x4, matrix products, one_block(): jnp.einsum('qhd,khd->hqk', grad_block, values, preferred_element_type=jnp...  51.3 us
    reduce_scatter x1, waiting for transfers between devices, on_device(): lax.psum_scatter(jnp.einsum('lrh,dh->lrd', part, w_project, preferred_ele...  48.6 us
    all_gather x1, waiting for transfers between devices, on_device(): piece = lax.all_gather(attn_input, 'head', axis=0, tiled=True)  48.6 us
    convert_element_type x4, other arithmetic, one_block(): score_grad = (probs * (weight_grad - jnp.sum(probs * weight_grad, axis=-1...  48.5 us
  transfers between devices with their start and end apart: 10, of which 9 were waited for; matrix products, arithmetic and copies ran while one was open for 31% of the time, Pallas kernels for 0%

commit v1 on v0

--- a/solution.py
+++ b/solution.py
@@ -1,6 +1,10 @@
+import functools
+
 import jax
 import jax.numpy as jnp
 from jax import lax
+from jax.experimental import pallas as pl
+from jax.experimental.pallas import tpu as pltpu
 from jax.sharding import PartitionSpec as P
 
 HEAD_DIM = 64
@@ -37,77 +41,154 @@
     )
 
 
-def by_rows(array, heads):
-    return jnp.moveaxis(array.reshape(array.shape[0], array.shape[1], heads, -1), 1, 0)
-
-
-def block_scores(queries, keys, segments, number, block):
-    length = keys.shape[0]
-    begin = number * block
-    query_block = lax.dynamic_slice_in_dim(queries, begin, block, 0)
-    query_index = begin + jnp.arange(block, dtype=jnp.int32)
-    key_index = jnp.arange(length, dtype=jnp.int32)
-    query_segments = lax.dynamic_slice_in_dim(segments, begin, block, 0)
-    allowed = (key_index[None, :] <= query_index[:, None]) & (
-        segments[None, :] == query_segments[:, None]
-    )
-    scores = jnp.einsum(
-        "qhd,khd->hqk", query_block, keys, preferred_element_type=jnp.float32
-    ) * HEAD_DIM ** (-0.5)
-    return (query_block, jnp.where(allowed[None], scores, masked_score))
-
-
-def attend_forward(queries, keys, values, segments, block):
-    length = queries.shape[0]
-
-    def one_block(carry, number):
-        query_block, scores = block_scores(queries, keys, segments, number, block)
-        top = jnp.max(scores, axis=-1, keepdims=True)
-        log_total = top + jnp.log(jnp.sum(jnp.exp(scores - top), axis=-1, keepdims=True))
-        weights = jnp.exp(scores - log_total).astype(jnp.bfloat16)
-        mixed = jnp.einsum("hqk,khd->qhd", weights, values, preferred_element_type=jnp.float32)
-        return (carry, (mixed, log_total))
-
-    _, (mixed, log_total) = lax.scan(one_block, 0, jnp.arange(length // block))
-    return (mixed.reshape(length, mixed.shape[2], mixed.shape[3]), log_total)
-
-
-def attend_backward(queries, keys, values, segments, mixed_grad, log_total, block):
-    length = queries.shape[0]
-    scale = HEAD_DIM ** (-0.5)
-
-    def one_block(carry, number):
-        key_grad, value_grad = carry
-        query_block, scores = block_scores(queries, keys, segments, number, block)
-        probs = jnp.exp(scores - log_total[number])
-        weights = probs.astype(jnp.bfloat16)
-        grad_block = lax.dynamic_slice_in_dim(mixed_grad, number * block, block, 0)
-        weight_grad = jnp.einsum(
-            "qhd,khd->hqk", grad_block, values, preferred_element_type=jnp.float32
-        )
-        score_grad = (
-            probs * (weight_grad - jnp.sum(probs * weight_grad, axis=-1, keepdims=True))
-        ).astype(jnp.bfloat16)
-        query_grad = (
-            jnp.einsum("hqk,khd->qhd", score_grad, keys, preferred_element_type=jnp.float32) * scale
-        )
-        key_grad = (
-            key_grad
-            + jnp.einsum(
-                "hqk,qhd->khd", score_grad, query_block, preferred_element_type=jnp.float32
-            )
-            * scale
-        )
-        value_grad = value_grad + jnp.einsum(
-            "hqk,qhd->khd", weights, grad_block, preferred_element_type=jnp.float32
-        )
-        return ((key_grad, value_grad), query_grad)
-
-    zeros = jnp.zeros(keys.shape, jnp.float32)
-    (key_grad, value_grad), query_grad = lax.scan(
-        one_block, (zeros, zeros), jnp.arange(length // block)
-    )
-    return (query_grad.reshape(keys.shape), key_grad, value_grad)
+NT=(((1,),(1,)),((),()))
+NN=(((1,),(0,)),((),()))
+TN=(((0,),(0,)),((),()))
+def dot(a,b,dims): return lax.dot_general(a,b,dims,preferred_element_type=jnp.float32)
+
+def head_lanes(lanes):
+    return lanes//HEAD_DIM
+
+def only_head(x,number,lanes,other=0.0):
+    if lanes==HEAD_DIM: return x
+    lane=lax.broadcasted_iota(jnp.int32,x.shape,1)
+    return jnp.where(lane//HEAD_DIM==number,x,jnp.asarray(other,x.dtype))
+
+def fwd2_kernel(block,firsts,lasts,q_ref,k_ref,v_ref,start_ref,o_ref,lse_ref,vt_ref):
+    i=pl.program_id(1)
+    length,lanes=k_ref.shape
+    heads=lanes//HEAD_DIM
+    @pl.when(i==0)
+    def _():
+        for r in range(length//block):
+            rows=pl.ds(r*block,block)
+            t=jnp.transpose(v_ref[rows,:])
+            for n in range(heads):
+                vt_ref[n,0:HEAD_DIM,rows]=t[n*HEAD_DIM:(n+1)*HEAD_DIM]
+                vt_ref[n,HEAD_DIM:,rows]=jnp.ones((16,block),jnp.bfloat16)
+    q=q_ref[...]*jnp.asarray(HEAD_DIM**-0.5,q_ref.dtype)
+    qs=[only_head(q,n,lanes) for n in range(heads)]
+    start=start_ref[...]
+    key=lax.broadcasted_iota(jnp.int32,(block,block),0)
+    col=i*block+lax.broadcasted_iota(jnp.int32,(block,block),1)
+    def step(masked,j,carry):
+        rows=pl.ds(pl.multiple_of(j*block,block),block)
+        k=k_ref[rows,:]
+        out=[]
+        if masked:
+            c=key+j*block
+            allowed=(c<=col)&(c>=start)
+        for n in range(heads):
+            m,acc=carry[n]
+            s=dot(k,qs[n],NT)
+            if masked: s=jnp.where(allowed,s,masked_score)
+            m_new=jnp.maximum(m,jnp.max(s,axis=0,keepdims=True))
+            p=jnp.exp(s-m_new).astype(jnp.bfloat16)
+            acc=acc*jnp.exp(m-m_new)+dot(vt_ref[n,:,rows],p,NN)
+            out.append((m_new,acc))
+        return tuple(out)
+    init=tuple((jnp.full((1,block),masked_score,jnp.float32),jnp.zeros((HEAD_DIM+16,block),jnp.float32)) for _ in range(heads))
+    a=firsts[i]//block
+    b=jnp.clip((lasts[i]+block-1)//block,a,i)
+    carry=lax.fori_loop(a,b,functools.partial(step,True),init)
+    carry=lax.fori_loop(b,i,functools.partial(step,False),carry)
+    carry=step(True,i,carry)
+    outs=[]
+    for n in range(heads):
+        m,acc=carry[n]
+        l=acc[HEAD_DIM:HEAD_DIM+1]
+        outs.append(acc[:HEAD_DIM]/l)
+        lse_ref[0,n:n+1,:]=m+jnp.log(l)
+    o=outs[0] if heads==1 else jnp.concatenate(outs,axis=0)
+    o_ref[...]=jnp.transpose(o).astype(o_ref.dtype)
+
+def attend_forward2(q,k,v,start,block):
+    length,width=q.shape
+    lanes=min(128,width); groups=width//lanes; nq=length//block
+    firsts=start[::block]; lasts=start[block-1::block]
+    spec=pltpu.PrefetchScalarGridSpec(num_scalar_prefetch=2,grid=(groups,nq),
+        in_specs=[pl.BlockSpec((block,lanes),lambda g,i,*_:(i,g)),
+                  pl.BlockSpec((length,lanes),lambda g,i,*_:(0,g)),
+                  pl.BlockSpec((length,lanes),lambda g,i,*_:(0,g)),
+                  pl.BlockSpec((1,block),lambda g,i,*_:(0,i))],
+        out_specs=[pl.BlockSpec((block,lanes),lambda g,i,*_:(i,g)),
+                   pl.BlockSpec((1,8,block),lambda g,i,*_:(g,0,i))],
+        scratch_shapes=[pltpu.VMEM((lanes//HEAD_DIM,HEAD_DIM+16,length),jnp.bfloat16)])
+    return pl.pallas_call(functools.partial(fwd2_kernel,block),grid_spec=spec,
+        out_shape=[jax.ShapeDtypeStruct((length,width),jnp.bfloat16),jax.ShapeDtypeStruct((groups,8,length),jnp.float32)],
+        compiler_params=pltpu.CompilerParams(vmem_limit_bytes=48*1024*1024),
+        cost_estimate=pl.CostEstimate(flops=4*length*length*width,bytes_accessed=8*length*width,transcendentals=length*length*width//HEAD_DIM),
+        name="attend_forward")(firsts,lasts,q,k,v,start[None,:])
+
+def backward_kernel(block,full_end,some_end,q_ref,k_ref,v_ref,d_ref,o_ref,lse_ref,start_ref,dq_ref,dk_ref,dv_ref,delta_ref):
+    j=pl.program_id(1)
+    length,lanes=q_ref.shape
+    heads=lanes//HEAD_DIM
+    @pl.when(j==0)
+    def _():
+        dq_ref[...]=jnp.zeros_like(dq_ref)
+        def fill(i,_):
+            rows=pl.ds(i*block,block)
+            prod=jnp.transpose(d_ref[rows,:].astype(jnp.float32)*o_ref[rows,:].astype(jnp.float32))
+            for n in range(heads):
+                delta_ref[n:n+1,rows]=jnp.sum(prod[n*HEAD_DIM:(n+1)*HEAD_DIM],axis=0,keepdims=True)
+            return 0
+        for i in range(length//block): fill(i,0)
+    k=k_ref[...]; v=v_ref[...]
+    scale=HEAD_DIM**-0.5
+    kl=[only_head(k,n,lanes) for n in range(heads)]
+    ks=[x*jnp.asarray(scale,k.dtype) for x in kl]
+    vs=[only_head(v,n,lanes) for n in range(heads)]
+    key=j*block+lax.broadcasted_iota(jnp.int32,(block,block),0)
+    col=lax.broadcasted_iota(jnp.int32,(block,block),1)
+    def step(masked,i,carry):
+        dk,dv=carry
+        rows=pl.ds(pl.multiple_of(i*block,block),block)
+        q=q_ref[rows,:]; d=d_ref[rows,:]
+        if masked:
+            allowed=(key<=col+i*block)&(key>=start_ref[0:1,rows])
+        dq=None; pk=[];pv=[]
+        for n in range(heads):
+            s=dot(ks[n],q,NT)
+            if masked: s=jnp.where(allowed,s,masked_score)
+            p=jnp.exp(s-lse_ref[0,n:n+1,rows])
+            dp=dot(vs[n],d,NT)
+            ds=(p*(dp-delta_ref[n:n+1,rows])).astype(jnp.bfloat16)
+            pv.append(dot(p.astype(jnp.bfloat16),d,NN))
+            pk.append(dot(ds,q,NN))
+            t=dot(ds,kl[n],TN)
+            dq=t if dq is None else dq+t
+        dq_ref[rows,:]+=dq*scale
+        if heads==2:
+            lane=lax.broadcasted_iota(jnp.int32,pv[0].shape,1)<HEAD_DIM
+            return dk+jnp.where(lane,pk[0],pk[1]),dv+jnp.where(lane,pv[0],pv[1])
+        return dk+pk[0],dv+pv[0]
+    zero=jnp.zeros((block,lanes),jnp.float32)
+    carry=step(True,j,(zero,zero))
+    carry=lax.fori_loop(j+1,full_end[j],functools.partial(step,False),carry)
+    carry=lax.fori_loop(full_end[j],some_end[j],functools.partial(step,True),carry)
+    dk_ref[...]=carry[0]*scale
+    dv_ref[...]=carry[1]
+
+def attend_backward(q,k,v,d,o,lse,start,block):
+    length,width=q.shape
+    lanes=min(128,width); groups=width//lanes; n=length//block
+    lasts=start[block-1::block]
+    edge=jnp.arange(n,dtype=jnp.int32)
+    full_end=jnp.maximum(edge+1,jnp.sum((lasts[None,:]<=edge[:,None]*block).astype(jnp.int32),axis=1))
+    reach=jnp.sum((start[None,:]<=edge[:,None]*block+block-1).astype(jnp.int32),axis=1)
+    some_end=jnp.maximum(full_end,(reach+block-1)//block)
+    whole=pl.BlockSpec((length,lanes),lambda g,j,*_:(0,g))
+    part=pl.BlockSpec((block,lanes),lambda g,j,*_:(j,g))
+    spec=pltpu.PrefetchScalarGridSpec(num_scalar_prefetch=2,grid=(groups,n),
+        in_specs=[whole,part,part,whole,whole,pl.BlockSpec((1,8,length),lambda g,j,*_:(g,0,0)),pl.BlockSpec((1,length),lambda g,j,*_:(0,0))],
+        out_specs=[whole,part,part],
+        scratch_shapes=[pltpu.VMEM((8,length),jnp.float32)])
+    return pl.pallas_call(functools.partial(backward_kernel,block),grid_spec=spec,
+        out_shape=[jax.ShapeDtypeStruct((length,width),jnp.float32)]*3,
+        compiler_params=pltpu.CompilerParams(vmem_limit_bytes=48*1024*1024),
+        cost_estimate=pl.CostEstimate(flops=10*length*length*width,bytes_accessed=22*length*width,transcendentals=length*length*width//HEAD_DIM),
+        name="attend_backward")(full_end,some_end,q,k,v,d,o,lse,start[None,:])
 
 
 def on_device(
@@ -157,16 +238,12 @@
             jnp.sum(jnp.sqrt(jnp.sum(blend_heads * blend_heads, axis=-1))),
         ]
     )
-    segment_rows = jnp.transpose(segment_ids, (1, 0))
-    query_rows = by_rows(queries, heads_here)
-    key_rows = by_rows(keys, heads_here)
-    value_rows = by_rows(blended_low, heads_here)
-
-    def forward_row(item):
-        return attend_forward(item[0], item[1], item[2], item[3], block)
-
-    mixed, log_total = lax.map(forward_row, (query_rows, key_rows, value_rows, segment_rows))
-    attn_mixed = jnp.moveaxis(mixed, 0, 1).reshape(length, rows_here, width).astype(jnp.bfloat16)
+    start = jnp.arange(length, dtype=jnp.int32) - positions[:, 0]
+    query_rows = queries[:, 0]
+    key_rows = keys[:, 0]
+    value_rows = blended_low[:, 0]
+    mixed, log_total = attend_forward2(query_rows, key_rows, value_rows, start, block)
+    attn_mixed = mixed[:, None]
     part = attn_mixed
     attn_branch = lax.psum_scatter(
         jnp.einsum("lrh,hd->lrd", part, w_out, preferred_element_type=jnp.float32),
@@ -217,19 +294,12 @@
     part_grad = jnp.einsum("lrd,hd->lrh", piece, w_out, preferred_element_type=jnp.float32)
     out_wgrad = out_sum
     mixed_grad_low = part_grad.astype(jnp.bfloat16)
-    mixed_grad_rows = by_rows(mixed_grad_low, heads_here)
-
-    def backward_row(item):
-        return attend_backward(item[0], item[1], item[2], item[3], item[4], item[5], block)
-
-    query_grad, key_grad, blend_grad = lax.map(
-        backward_row, (query_rows, key_rows, value_rows, segment_rows, mixed_grad_rows, log_total)
-    )
-    query_grad = jnp.moveaxis(query_grad, 0, 1)
-    key_grad = jnp.moveaxis(key_grad, 0, 1)
-    blend_low = (
-        jnp.moveaxis(blend_grad, 0, 1).reshape(length, rows_here, width).astype(jnp.bfloat16)
-    )
+    query_grad, key_grad, blend_grad = attend_backward(
+        query_rows, key_rows, value_rows, mixed_grad_low[:, 0], mixed, log_total, start, block
+    )
+    query_grad = query_grad.reshape(length, rows_here, heads_here, HEAD_DIM)
+    key_grad = key_grad.reshape(length, rows_here, heads_here, HEAD_DIM)
+    blend_low = blend_grad[:, None].astype(jnp.bfloat16)
     query_pre = (
         rotate(query_grad, positions, -1.0).reshape(length, rows_here, width).astype(jnp.bfloat16)
     )

time: 1070 us -> 847 us (0.79)
  matrix products: 241 us -> 84.8 us
  other arithmetic: 130 us -> 55.7 us
  Pallas kernels: 0 us -> 69.1 us
  local copies, waits for them, and re-layouts: 117 us -> 50.2 us
  waiting for transfers between devices: 503 us -> 517 us
  loops' own time: 12.4 us -> 0 us
    dot_general x28 -> x0, matrix products: 158 us -> none  [the longest x4 51.3 us: one_block(): jnp.einsum('qhd,khd->hqk', grad_block, values, preferred_element_type=jnp...]
    pallas_call x0 -> x2, Pallas kernels: none -> 69.1 us  [the longest x1 42.1 us: attend_backward(): pl.pallas_call(functools.partial(backward_kernel, block), grid_spec=spec,...]
    convert_element_type x5 -> x0, other arithmetic: 48.7 us -> none  [the longest x4 48.5 us: one_block(): score_grad = (probs * (weight_grad - jnp.sum(probs * weight_grad, axis=-1...]
    dynamic_update_slice x8 -> x0, local copies, waits for them, and re-layouts: 46.6 us -> none  [attend_forward(): _, (mixed, log_total) = lax.scan(one_block, 0, jnp.arange(length // block))]
    while x24 -> x0, local copies, waits for them, and re-layouts: 27.1 us -> none
    psum x1, waiting for transfers between devices: 33.1 us -> 51.7 us  [on_device(): lax.psum(proj_wgrad[:, :width].astype(jnp.bfloat16), ('dp', 'mlp'))]
    reduce_sum x4 -> x2, other arithmetic: 17.3 us -> 1.08 us  [the longest x1 0.9 us: attend_backward(): jnp.sum((start[None, :] <= edge[:, None] * block + block - 1).astype(jnp....]
    another operation x2 -> x0, loops' own time: 12.4 us -> none  [the longest x1 9.48 us: attend_backward(): lax.scan(one_block, (zeros, zeros), jnp.arange(length // block))]
  transfers between devices with their start and end apart: 10 -> 10, of which waited for: 9 -> 9; matrix products, arithmetic and copies ran while one was open for 31% -> 13% of each run, Pallas kernels for 0% -> 5%
where the time goes in v1:
time: 847 us; the launch traced here: 838 us
  waiting for transfers between devices  517 us (61%)
  matrix products  84.8 us (10%)
  Pallas kernels  69.1 us (8%)
  other arithmetic  55.7 us (7%)
  local copies, waits for them, and re-layouts  50.2 us (6%)
  blocking collectives  45 us (5%)
  between operations  14.8 us (2%)
    reduce_scatter x1, waiting for transfers between devices, on_device(): lax.psum_scatter(jnp.einsum('lrh,hd->lrd', part, w_out, preferred_element...  83.7 us
    reduce_scatter x1, waiting for transfers between devices, on_device(): lax.psum_scatter(input_terms.astype(jnp.bfloat16), 'mlp', scatter_dimensi...  74.9 us
    all_gather x1, waiting for transfers between devices, on_device(): piece = lax.all_gather(mlp_input, 'mlp', axis=1, tiled=True)  74.8 us
    all_gather x1, waiting for transfers between devices, on_device(): piece = lax.all_gather(out_grad, 'mlp', axis=1, tiled=True)  67.6 us
    psum x1, waiting for transfers between devices, on_device(): lax.psum(proj_wgrad[:, :width].astype(jnp.bfloat16), ('dp', 'mlp'))  51.7 us
    all_gather x1, waiting for transfers between devices, on_device(): piece = lax.all_gather(attn_input, 'head', axis=0, tiled=True)  51.6 us
    reduce_scatter x1, waiting for transfers between devices, on_device(): lax.psum_scatter(jnp.einsum('lrh,dh->lrd', part, w_project, preferred_ele...  48.7 us
    psum x1, blocking collectives, on_device(): lax.psum((attn_gain_grad, mlp_gain_grad, norm_local), ('dp', 'head', 'mlp'))  45 us
  transfers between devices with their start and end apart: 10, of which 9 were waited for; matrix products, arithmetic and copies ran while one was open for 13% of the time, Pallas kernels for 5%

profile of v1, /device:TPU:0, one launch (start us, length us, event | category | flops | bytes accessed | tf_op | source)
XLA Modules:
  0.0 838.2 jit_solution(4067688542066210836)
XLA Ops:
  9.5 2.6 fusion.21
  16.0 51.6 %all-gather.5.cloned.1.call-done = bf16[2048,1,1024]{2,0,1:T(8,128)(2,1)} async-done(((bf16[512,1,1024]{2,0,1:T(8,128)(2,1)}), bf16[2048,1,1024]{2,0,1:T(8,128)(2,1)}) %all-gather.5.cloned.1.call-update) | async-done | bytes 4194320 | tf_op jit(solution)/shard_map/all_gather | solution.py:220
  67.6 5.7 fusion.8
  73.4 3.5 fusion.47
  76.8 2.9 copy.104
  79.7 2.9 copy.103
  82.6 2.8 subtract_convert_fusion.2
  86.6 2.3 copy.105.q_ref
  92.6 27.0 %attend_forward.1 = (bf16[2048,256]{1,0:T(8,128)(2,1)S(1)}, f32[2,8,2048]{2,1,0:T(8,128)S(1)}) custom-call(s32[4]{0:T(128)S(1)} %slice.66.firsts, s32[4]{0:T(128)S(1)} %slice.67.lasts, bf16[2048,256]{1,0:T(8,128)(2,1)S(1)} %copy-done.1, bf16[2048,256]{1,0:T(8,128)(2,1)S(1)} %copy-done.3, bf16[2048,256]{1,0:T(8,128)(2,1)S(1)} %get-tuple-element.108.v_ref, ...), custom_call_target="tpu_custom_call" | custom-call | flops 4294967296 | bytes 4194304 | tf_op jit(solution)/shard_map/attend_forward/pallas_call | solution.py:117
  120.2 4.5 convolution_bitcast_fusion
  124.9 83.7 %reduce-scatter.5.cloned.1.call-done = f32[512,1,1024]{2,0,1:T(8,128)} async-done(((f32[2048,1,1024]{2,0,1:T(8,128)}), f32[512,1,1024]{2,0,1:T(8,128)}) %reduce-scatter.5.cloned.1.call-update) | async-done | bytes 2097168 | tf_op jit(solution)/shard_map/reduce_scatter | solution.py:248
  208.6 2.2 multiply_reduce_fusion
  214.4 2.6 copy.107
  217.0 2.6 copy.108
  219.6 74.8 %all-gather.7.cloned.1.call-done = bf16[512,4,1024]{2,0,1:T(8,128)(2,1)} async-done(((bf16[512,1,1024]{2,0,1:T(8,128)(2,1)}), bf16[512,4,1024]{2,0,1:T(8,128)(2,1)}) %all-gather.7.cloned.1.call-update) | async-done | bytes 4194320 | tf_op jit(solution)/shard_map/all_gather | solution.py:258
  294.4 13.2 %fusion.37 = f32[512,4,1408]{0,2,1:T(8,128)} fusion(bf16[512,4,1024]{2,0,1:T(8,128)(2,1)} %all-gather.7.cloned.1.call-done, bf16[1024,704]{1,0:T(8,128)(2,1)} %copy.108, bf16[1024,704]{1,0:T(8,128)(2,1)} %copy.107), kind=kOutput, calls=%fused_computation.59 | convolution fusion | flops 5911347200 | bytes 18612224 | tf_op jit(solution)/shard_map/lrd,df->lrf/dot_general | solution.py:259
  307.6 67.6 %all-gather.9.cloned.1.call-done = bf16[512,4,1024]{2,0,1:T(8,128)(2,1)} async-done(((bf16[512,1,1024]{2,0,1:T(8,128)(2,1)}), bf16[512,4,1024]{2,0,1:T(8,128)(2,1)}) %all-gather.9.cloned.1.call-update) | async-done | bytes 4194320 | tf_op jit(solution)/shard_map/all_gather | solution.py:271
  375.2 10.6 %multiply_convert_fusion.1 = (bf16[512,4,704]{0,2,1:T(8,128)(2,1)S(1)}, bf16[512,4,704]{0,2,1:T(8,128)(2,1)S(1)}, bf16[512,4,704]{0,2,1:T(8,128)(2,1)}) fusion(f32[512,4,1408]{0,2,1:T(8,128)} %fusion.37, bf16[512,4,1024]{2,0,1:T(8,128)(2,1)} %all-gather.9.cloned.1.call-done, bf16[704,1024]{1,0:T(8,128)(2,1)S(1)} %copy-done), kind=kOutput, calls=%fused_computation.3 | convolution fusion | flops 2975858688 | bytes 25821184 | tf_op jit(solution)/shard_map/lrd,fd->lrf/dot_general | solution.py:273
  388.3 9.5 %fusion.12 = bf16[512,4,1024]{2,0,1:T(8,128)(2,1)} fusion(bf16[512,4,704]{0,2,1:T(8,128)(2,1)S(1)} %get-tuple-element.105, bf16[512,4,704]{0,2,1:T(8,128)(2,1)S(1)} %get-tuple-element.104, bf16[1024,704]{1,0:T(8,128)(2,1)S(1)} %copy-done.15, bf16[1024,704]{1,0:T(8,128)(2,1)S(1)} %copy-done.14), kind=kOutput, calls=%fused_computation.26 | convolution fusion | flops 5924978688 | bytes 12845056 | tf_op jit(solution)/shard_map/lrf,df->lrd/dot_general | solution.py:283
  398.4 74.9 %reduce-scatter.9.cloned.1.call-done = bf16[512,1,1024]{2,0,1:T(8,128)(2,1)} async-done(((bf16[512,4,1024]{2,0,1:T(8,128)(2,1)}), bf16[512,1,1024]{2,0,1:T(8,128)(2,1)}) %reduce-scatter.9.cloned.1.call-update) | async-done | bytes 1048592 | tf_op jit(solution)/shard_map/reduce_scatter | solution.py:286
  473.2 3.4 fusion.32
  477.1 3.0 fusion.57
  481.3 10.4 %bitcast_convert_fusion = bf16[1024,1408]{1,0:T(8,128)(2,1)S(1)} fusion(bf16[512,4,1024]{2,0,1:T(8,128)(2,1)} %all-gather.7.cloned.1.call-done, bf16[512,4,704]{0,2,1:T(8,128)(2,1)} %copy-done.44, bf16[512,4,704]{0,2,1:T(8,128)(2,1)} %copy-done.43), kind=kOutput, calls=%fused_computation.1 | convolution fusion | flops 5918556160 | bytes 12845056 | tf_op jit(solution)/shard_map/lrd,lrf->df/dot_general | solution.py:280
  491.8 2.4 fusion.58
  495.1 4.3 bitcast_convert_fusion.1
  499.6 33.9 %all-gather.11.cloned.1.call-done = bf16[2048,1,1024]{2,0,1:T(8,128)(2,1)} async-done(((bf16[512,1,1024]{2,0,1:T(8,128)(2,1)}), bf16[2048,1,1024]{2,0,1:T(8,128)(2,1)}) %all-gather.11.cloned.1.call-update) | async-done | bytes 4194320 | tf_op jit(solution)/shard_map/all_gather | solution.py:292
  533.5 3.7 fusion.13.d_ref
  537.3 42.1 %attend_backward.1 = (f32[2048,256]{1,0:T(8,128)}, f32[2048,256]{1,0:T(8,128)}, f32[2048,256]{1,0:T(8,128)}) custom-call(s32[4]{0:T(128)S(1)} %get-tuple-element.135.full_end, s32[4]{0:T(128)S(1)} %get-tuple-element.134.some_end, bf16[2048,256]{1,0:T(8,128)(2,1)S(1)} %copy-done.2, bf16[2048,256]{1,0:T(8,128)(2,1)S(1)} %copy-done.4, ...), custom_call_target="tpu_custom_call" | custom-call | flops 10737418240 | bytes 11534336 | tf_op jit(solution)/shard_map/attend_backward/pallas_call | solution.py:187
  579.4 3.0 copy.114
  582.4 2.9 copy.115
  585.3 3.1 subtract_convert_fusion.1
  590.9 2.4 copy.117
  595.5 6.2 fusion.38
  602.9 2.1 fusion.44
  606.2 7.3 convert_bitcast_fusion
  613.5 7.3 convolution_convert_fusion
  622.8 2.9 copy.120
  631.4 3.1 copy.122
  634.5 2.0 copy.123
  636.4 3.3 convert_element_type.198
  639.7 51.7 %all-reduce.6.cloned.1.call-done = (bf16[1024,256]{1,0:T(8,128)(2,1)}, bf16[1024,256]{1,0:T(8,128)(2,1)}, bf16[1024,256]{1,0:T(8,128)(2,1)}, bf16[256,1024]{1,0:T(8,128)(2,1)}) async-done(((bf16[1024,256]{1,0:T(8,128)(2,1)}, bf16[1024,256]{1,0:T(8,128)(2,1)}, bf16[1024,256]{1,0:T(8,128)(2,1)}, bf16[256,1024]{1,0:T(8,128)(2,1)}), (bf16[1024,256]{1,0:T(8,128)(2,1)}, bf16[1024,256]{1,0:T(8,128)(2,1)}, ...) | async-done | bytes 2097168 | tf_op jit(solution)/shard_map/psum | solution.py:325
  691.5 2.2 convert_element_type.190
  693.7 2.1 convert_element_type.191
  697.9 48.7 %reduce-scatter.11.cloned.1.call-done = bf16[512,1,1024]{2,0,1:T(8,128)(2,1)} async-done(((bf16[2048,1,1024]{2,0,1:T(8,128)(2,1)}), bf16[512,1,1024]{2,0,1:T(8,128)(2,1)}) %reduce-scatter.11.cloned.1.call-update) | async-done | bytes 1048592 | tf_op jit(solution)/shard_map/reduce_scatter | solution.py:314
  746.6 3.0 fusion.36
  749.6 45.0 %all-reduce = (f32[1024]{0:T(1024)}, f32[1024]{0:T(1024)}, f32[2]{0:T(128)}) all-reduce(f32[1024]{0:T(1024)} %get-tuple-element.90, f32[1024]{0:T(1024)} %get-tuple-element.88, f32[2]{0:T(128)} %pad_maximum_fusion.9), channel_id=1, replica_groups=mesh['dp'=2,'head'=4,'mlp'=4] {'dp','head','mlp'}, use_global_device_ids=true, to_apply=%region_11.12 | all-reduce | flops 2050 | bytes 16400 | tf_op jit(solution)/shard_map/psum | solution.py:343
  797.1 29.6 %reduce-scatter.7.cloned.1.call-done = bf16[512,1,1024]{2,0,1:T(8,128)(2,1)} async-done(((bf16[512,4,1024]{2,0,1:T(8,128)(2,1)}), bf16[512,1,1024]{2,0,1:T(8,128)(2,1)}) %reduce-scatter.7.cloned.1.call-update) | async-done | bytes 1048592 | tf_op jit(solution)/shard_map/reduce_scatter | solution.py:267
  826.7 4.4 fusion.26
  (148 shorter events, 40.6 us)
Async XLA Ops:
  7.2 368.0 %copy-start = (bf16[704,1024]{1,0:T(8,128)(2,1)S(1)}, bf16[704,1024]{1,0:T(8,128)(2,1)}, u32[]{:S(2)}) copy-start(bf16[704,1024]{1,0:T(8,128)(2,1)} %param.25) | copy-start | bytes 4325380
  7.2 4.9 copy-start.30
  7.2 5.7 copy-start.25
  7.2 60.4 %all-gather.5.cloned.1.call-start = ((), (), s32[]{:S(2)}) async-start(), calls=%async_computation.4 | async-start | bytes 5242880 | tf_op jit(solution)/shard_map/all_gather | solution.py:220
  9.5 3.4 copy-start.26
  12.1 196.5 %reduce-scatter.5.cloned.1.call-start = ((), (), s32[]{:S(2)}) async-start(), calls=%async_computation.5 | async-start | bytes 10485760 | tf_op jit(solution)/shard_map/reduce_scatter | solution.py:248
  16.0 66.6 %copy-start.11 = (f32[2048,32]{0,1:T(8,128)}, f32[2048,32]{0,1:T(8,128)S(1)}, u32[]{:S(2)}) copy-start(f32[2048,32]{0,1:T(8,128)S(1)} %get-tuple-element.133) | copy-start | bytes 786436
  67.6 5.7 copy-start.16
  90.1 1.2 copy-start.1
  91.4 1.2 copy-start.3
  92.6 27.7 %copy-start.22 = (bf16[256,1024]{1,0:T(8,128)(2,1)S(1)}, bf16[256,1024]{1,0:T(8,128)(2,1)}, u32[]{:S(2)}) copy-start(bf16[256,1024]{1,0:T(8,128)(2,1)} %param.21) | copy-start | bytes 1572868
  124.8 87.4 %copy-start.31 = (f32[1024]{0:T(1024)S(1)}, f32[1024]{0:T(1024)}, u32[]{:S(2)}) copy-start(f32[1024]{0:T(1024)} %param.22) | copy-start | bytes 12292
  124.8 169.5 %all-gather.7.cloned.1.call-start = ((), (), s32[]{:S(2)}) async-start(), calls=%async_computation.6 | async-start | bytes 5242880 | tf_op jit(solution)/shard_map/all_gather | solution.py:258
  210.8 1.4 copy-start.7
  210.8 1.4 copy-start.33
  213.4 161.7 %all-gather.9.cloned.1.call-start = ((), (), s32[]{:S(2)}) async-start(), calls=%async_computation.8 | async-start | bytes 5242880 | tf_op jit(solution)/shard_map/all_gather | solution.py:271
  214.0 259.2 %reduce-scatter.9.cloned.1.call-start = ((), (), s32[]{:S(2)}) async-start(), calls=%async_computation.9 | async-start | bytes 5242880 | tf_op jit(solution)/shard_map/reduce_scatter | solution.py:286
  375.2 13.1 %copy-start.14 = (bf16[1024,704]{1,0:T(8,128)(2,1)S(1)}, bf16[1024,704]{1,0:T(8,128)(2,1)}, u32[]{:S(2)}) copy-start(bf16[1024,704]{1,0:T(8,128)(2,1)} %copy.107) | copy-start | bytes 4325380
  375.2 13.1 %copy-start.15 = (bf16[1024,704]{1,0:T(8,128)(2,1)S(1)}, bf16[1024,704]{1,0:T(8,128)(2,1)}, u32[]{:S(2)}) copy-start(bf16[1024,704]{1,0:T(8,128)(2,1)} %copy.108) | copy-start | bytes 4325380
  385.8 1.6 copy-start.43
  385.8 2.5 copy-start.44
  397.8 135.7 %all-gather.11.cloned.1.call-start = ((), (), s32[]{:S(2)}) async-start(), calls=%async_computation.10 | async-start | bytes 5242880 | tf_op jit(solution)/shard_map/all_gather | solution.py:292
  473.2 3.9 copy-start.8
  473.2 3.9 copy-start.10
  480.2 151.2 %all-reduce.8.cloned.1.call-start = ((), (), s32[]{:S(2)}) async-start(), calls=%async_computation.13 | async-start | bytes 9175040 | tf_op jit(solution)/shard_map/psum | solution.py:335
  481.3 12.8 %copy-start.42 = (bf16[512,4,704]{0,2,1:T(8,128)(2,1)S(1)}, bf16[512,4,704]{0,2,1:T(8,128)(2,1)}, u32[]{:S(2)}) copy-start(bf16[512,4,704]{0,2,1:T(8,128)(2,1)} %get-tuple-element.106) | copy-start | bytes 8650756
  491.8 3.3 copy-start.41
  499.4 192.1 %all-reduce.6.cloned.1.call-start = ((), (), s32[]{:S(2)}) async-start(), calls=%async_computation.12 | async-start | bytes 4194304 | tf_op jit(solution)/shard_map/psum | solution.py:325
  533.5 3.8 copy-start.2
  533.5 3.8 copy-start.4
  533.5 3.8 copy-start.6
  582.4 2.9 copy-start.12
  582.4 2.9 copy-start.21
  593.3 1.9 copy-start.18
  593.3 2.2 copy-start.20
  595.5 9.5 %copy-start.17 = (bf16[2048,1,256]{2,0,1:T(8,128)(2,1)}, bf16[2048,1,256]{2,0,1:T(8,128)(2,1)S(1)}, u32[]{:S(2)}) copy-start(bf16[2048,1,256]{2,0,1:T(8,128)(2,1)S(1)} %fusion.50) | copy-start | bytes 3145732
  595.5 7.4 copy-start.40
  605.0 141.6 %reduce-scatter.11.cloned.1.call-start = ((), (), s32[]{:S(2)}) async-start(), calls=%async_computation.11 | async-start | bytes 5242880 | tf_op jit(solution)/shard_map/reduce_scatter | solution.py:314
  613.5 213.2 %reduce-scatter.7.cloned.1.call-start = ((), (), s32[]{:S(2)}) async-start(), calls=%async_computation.7 | async-start | bytes 5242880 | tf_op jit(solution)/shard_map/reduce_scatter | solution.py:267
  626.5 1.8 copy-start.29
  631.4 3.1 copy-start.13
  691.5 4.3 copy-start.24
  691.5 5.4 copy-start.23
  693.7 53.0 %copy-start.35 = (f32[1024]{0:T(1024)S(1)}, f32[1024]{0:T(1024)}, u32[]{:S(2)}) copy-start(f32[1024]{0:T(1024)} %param.17) | copy-start | bytes 12292
  693.7 53.0 %copy-start.38 = (f32[512]{0:T(512)S(1)}, f32[512]{0:T(512)}, u32[]{:S(2)}) copy-start(f32[512]{0:T(512)} %copy-done.37) | copy-start | bytes 6148
  696.8 129.9 %copy-start.9 = (f32[512,1,1024]{2,0,1:T(8,128)S(1)}, f32[512,1,1024]{2,0,1:T(8,128)}, u32[]{:S(2)}) copy-start(f32[512,1,1024]{2,0,1:T(8,128)} %copy-done.7) | copy-start | bytes 6291460
  696.8 129.9 %copy-start.32 = (f32[1024]{0:T(1024)S(1)}, f32[1024]{0:T(1024)}, u32[]{:S(2)}) copy-start(f32[1024]{0:T(1024)} %param.22) | copy-start | bytes 12292
  696.8 129.9 %copy-start.34 = (f32[512]{0:T(512)S(1)}, f32[512]{0:T(512)}, u32[]{:S(2)}) copy-start(f32[512]{0:T(512)} %copy-done.33) | copy-start | bytes 6148
  (7 other events, 5.8 us)
Sparse Core Ops, SparseCore 0:
  12.2 55.3 all-gather.4
  124.9 83.6 reduce-scatter.4
  213.6 80.7 all-gather.6
  295.9 79.2 all-gather.8
  397.9 75.2 reduce-scatter.8
  480.3 53.1 all-gather.10
  537.2 85.7 all-reduce.7
  626.2 65.2 all-reduce.5
  694.5 52.1 reduce-scatter.10
  748.9 77.7 reduce-scatter.6

commit v2 on v1

v2 whole, which is shorter than its diff:
```python
import functools

import jax
import jax.numpy as jnp
from jax import lax
from jax.experimental import pallas as pl
from jax.experimental.pallas import tpu as pltpu
from jax.sharding import PartitionSpec as P

HEAD_DIM = 64
epsilon = 1e-06
theta_base = 10000.0
blend_weight = 0.5
masked_score = -1e30
NT=(((1,),(1,)),((),()))
NN=(((1,),(0,)),((),()))
TN=(((0,),(0,)),((),()))
def dot(a,b,dims): return lax.dot_general(a,b,dims,preferred_element_type=jnp.float32)

def head_lanes(lanes):
    return lanes//HEAD_DIM

def only_head(x,number,lanes,other=0.0):
    if lanes==HEAD_DIM: return x
    lane=lax.broadcasted_iota(jnp.int32,x.shape,1)
    return jnp.where(lane//HEAD_DIM==number,x,jnp.asarray(other,x.dtype))

def fwd2_kernel(block,firsts,lasts,q_ref,k_ref,v_ref,start_ref,o_ref,lse_ref,vt_ref):
    i=pl.program_id(1)
    length,lanes=k_ref.shape
    heads=lanes//HEAD_DIM
    @pl.when(i==0)
    def _():
        for r in range(length//block):
            rows=pl.ds(r*block,block)
            t=jnp.transpose(v_ref[rows,:])
            for n in range(heads):
                vt_ref[n,0:HEAD_DIM,rows]=t[n*HEAD_DIM:(n+1)*HEAD_DIM]
                vt_ref[n,HEAD_DIM:,rows]=jnp.ones((16,block),jnp.bfloat16)
    q=q_ref[...]*jnp.asarray(HEAD_DIM**-0.5,q_ref.dtype)
    qs=[only_head(q,n,lanes) for n in range(heads)]
    start=start_ref[...]
    key=lax.broadcasted_iota(jnp.int32,(block,block),0)
    col=i*block+lax.broadcasted_iota(jnp.int32,(block,block),1)
    def step(masked,j,carry):
        rows=pl.ds(pl.multiple_of(j*block,block),block)
        k=k_ref[rows,:]
        out=[]
        if masked:
            c=key+j*block
            allowed=(c<=col)&(c>=start)
        for n in range(heads):
            m,acc=carry[n]
            s=dot(k,qs[n],NT)
            if masked: s=jnp.where(allowed,s,masked_score)
            m_new=jnp.maximum(m,jnp.max(s,axis=0,keepdims=True))
            p=jnp.exp(s-m_new).astype(jnp.bfloat16)
            acc=acc*jnp.exp(m-m_new)+dot(vt_ref[n,:,rows],p,NN)
            out.append((m_new,acc))
        return tuple(out)
    init=tuple((jnp.full((1,block),masked_score,jnp.float32),jnp.zeros((HEAD_DIM+16,block),jnp.float32)) for _ in range(heads))
    a=firsts[i]//block
    b=jnp.clip((lasts[i]+block-1)//block,a,i)
    carry=lax.fori_loop(a,b,functools.partial(step,True),init)
    carry=lax.fori_loop(b,i,functools.partial(step,False),carry)
    carry=step(True,i,carry)
    outs=[]
    for n in range(heads):
        m,acc=carry[n]
        l=acc[HEAD_DIM:HEAD_DIM+1]
        outs.append(acc[:HEAD_DIM]/l)
        lse_ref[0,n:n+1,:]=m+jnp.log(l)
    o=outs[0] if heads==1 else jnp.concatenate(outs,axis=0)
    o_ref[...]=jnp.transpose(o).astype(o_ref.dtype)

def attend_forward2(q,k,v,start,block):
    length,width=q.shape
    lanes=min(128,width); groups=width//lanes; nq=length//block
    firsts=start[::block]; lasts=start[block-1::block]
    spec=pltpu.PrefetchScalarGridSpec(num_scalar_prefetch=2,grid=(groups,nq),
        in_specs=[pl.BlockSpec((block,lanes),lambda g,i,*_:(i,g)),
                  pl.BlockSpec((length,lanes),lambda g,i,*_:(0,g)),
                  pl.BlockSpec((length,lanes),lambda g,i,*_:(0,g)),
                  pl.BlockSpec((1,block),lambda g,i,*_:(0,i))],
        out_specs=[pl.BlockSpec((block,lanes),lambda g,i,*_:(i,g)),
                   pl.BlockSpec((1,8,block),lambda g,i,*_:(g,0,i))],
        scratch_shapes=[pltpu.VMEM((lanes//HEAD_DIM,HEAD_DIM+16,length),jnp.bfloat16)])
    return pl.pallas_call(functools.partial(fwd2_kernel,block),grid_spec=spec,
        out_shape=[jax.ShapeDtypeStruct((length,width),jnp.bfloat16),jax.ShapeDtypeStruct((groups,8,length),jnp.float32)],
        compiler_params=pltpu.CompilerParams(vmem_limit_bytes=48*1024*1024),
        cost_estimate=pl.CostEstimate(flops=24*length*length*width,bytes_accessed=8*length*width,transcendentals=0),
        name="attend_forward")(firsts,lasts,q,k,v,start[None,:])

def backward_kernel(block,full_end,some_end,q_ref,k_ref,v_ref,d_ref,o_ref,lse_ref,start_ref,*rest):
    dq_ref,dk_ref,dv_ref,delta_ref=rest[-4:]
    j=pl.program_id(1)
    length,lanes=q_ref.shape
    heads=lanes//HEAD_DIM
    @pl.when(j==0)
    def _():
        dq_ref[...]=jnp.zeros_like(dq_ref)
        def fill(i,_):
            rows=pl.ds(i*block,block)
            prod=jnp.transpose(d_ref[rows,:].astype(jnp.float32)*o_ref[rows,:].astype(jnp.float32))
            for n in range(heads):
                delta_ref[n:n+1,rows]=jnp.sum(prod[n*HEAD_DIM:(n+1)*HEAD_DIM],axis=0,keepdims=True)
            return 0
        for i in range(length//block): fill(i,0)
    k=k_ref[...]; v=v_ref[...]
    scale=HEAD_DIM**-0.5
    kl=[only_head(k,n,lanes) for n in range(heads)]
    ks=[x*jnp.asarray(scale,k.dtype) for x in kl]
    vs=[only_head(v,n,lanes) for n in range(heads)]
    key=j*block+lax.broadcasted_iota(jnp.int32,(block,block),0)
    col=lax.broadcasted_iota(jnp.int32,(block,block),1)
    def step(masked,i,carry):
        dk,dv=carry
        rows=pl.ds(pl.multiple_of(i*block,block),block)
        q=q_ref[rows,:]; d=d_ref[rows,:]
        if masked:
            allowed=(key<=col+i*block)&(key>=start_ref[0:1,rows])
        dq=None; pk=[];pv=[]
        for n in range(heads):
            s=dot(ks[n],q,NT)
            if masked: s=jnp.where(allowed,s,masked_score)
            p=jnp.exp(s-lse_ref[0,n:n+1,rows])
            dp=dot(vs[n],d,NT)
            ds=(p*(dp-delta_ref[n:n+1,rows])).astype(jnp.bfloat16)
            pv.append(dot(p.astype(jnp.bfloat16),d,NN))
            pk.append(dot(ds,q,NN))
            t=dot(ds,kl[n],TN)
            dq=t if dq is None else dq+t
        dq_ref[rows,:]+=dq*scale
        if heads==2:
            lane=lax.broadcasted_iota(jnp.int32,pv[0].shape,1)<HEAD_DIM
            return dk+jnp.where(lane,pk[0],pk[1]),dv+jnp.where(lane,pv[0],pv[1])
        return dk+pk[0],dv+pv[0]
    zero=jnp.zeros((block,lanes),jnp.float32)
    carry=step(True,j,(zero,zero))
    carry=lax.fori_loop(j+1,full_end[j],functools.partial(step,False),carry)
    carry=lax.fori_loop(full_end[j],some_end[j],functools.partial(step,True),carry)
    dk_ref[...]=carry[0]*scale
    dv_ref[...]=carry[1]

def attend_backward(q,k,v,d,o,lse,start,block,group,earlier=()):
    length,width=q.shape
    lanes=min(128,width); n=length//block
    lasts=start[block-1::block]
    edge=jnp.arange(n,dtype=jnp.int32)
    full_end=jnp.maximum(edge+1,jnp.sum((lasts[None,:]<=edge[:,None]*block).astype(jnp.int32),axis=1))
    reach=jnp.sum((start[None,:]<=edge[:,None]*block+block-1).astype(jnp.int32),axis=1)
    some_end=jnp.maximum(full_end,(reach+block-1)//block)
    whole=pl.BlockSpec((length,lanes),lambda g,j,*_:(0,group))
    part=pl.BlockSpec((block,lanes),lambda g,j,*_:(j,group))
    spec=pltpu.PrefetchScalarGridSpec(num_scalar_prefetch=2,grid=(1,n),
        in_specs=[whole,part,part,whole,whole,pl.BlockSpec((1,8,length),lambda g,j,*_:(group,0,0)),pl.BlockSpec((1,length),lambda g,j,*_:(0,0))]+[pl.BlockSpec(memory_space=pl.ANY)]*len(earlier),
        out_specs=[pl.BlockSpec((length,lanes),lambda g,j,*_:(0,0))]+[pl.BlockSpec((block,lanes),lambda g,j,*_:(j,0))]*2,
        scratch_shapes=[pltpu.VMEM((8,length),jnp.float32)])
    return pl.pallas_call(functools.partial(backward_kernel,block),grid_spec=spec,
        out_shape=[jax.ShapeDtypeStruct((length,lanes),jnp.float32)]*3,
        compiler_params=pltpu.CompilerParams(vmem_limit_bytes=48*1024*1024),
        cost_estimate=pl.CostEstimate(flops=36*length*length*lanes,bytes_accessed=22*length*lanes,transcendentals=0),
        name="attend_backward")(full_end,some_end,q,k,v,d,o,lse,start[None,:],*earlier)


f32 = jnp.float32
bf16 = jnp.bfloat16
everywhere = pl.BlockSpec(memory_space=pl.ANY)


def swap(x, axis, mask):
    return lax.ppermute(x, axis, [(i, i ^ mask) for i in range(lax.axis_size(axis))])


def cut_of(rows):
    half = rows // 2
    return half - half % 8 if half >= 8 else half


def after(x, *earlier):
    def kernel(*refs):
        pass

    return pl.pallas_call(
        kernel,
        in_specs=[everywhere] * (1 + len(earlier)),
        out_specs=everywhere,
        out_shape=jax.ShapeDtypeStruct(x.shape, x.dtype),
        input_output_aliases={0: 0},
        name="after",
    )(x, *earlier)


def spread_relay(x, axis):
    count = lax.axis_size(axis)
    if count != 4:
        return [[x]] + [[swap(x, axis, e)] for e in range(1, count)]
    cut = cut_of(x.shape[0])
    one, two = swap(x, axis, 1), swap(x, axis, 2)
    return [[x], [one], [two], [swap(two[:cut], axis, 1), swap(one[cut:], axis, 2)]]


def spread(x, axis):
    return [x] + [swap(x, axis, e) for e in range(1, lax.axis_size(axis))]


def add_low(*terms):
    return sum(t.astype(f32) for t in terms).astype(bf16)


def collect(parts, axis):
    return sum((swap(p, axis, e) if e else p).astype(f32) for e, p in enumerate(parts))


def collect_relay(parts, axis, earlier):
    if lax.axis_size(axis) != 4:
        return collect(parts, axis), parts[0]
    own, one, two, three = parts
    cut = cut_of(own.shape[0])
    for_two = swap(three[:cut], axis, 1)
    for_one = swap(three[cut:], axis, 2)
    for_one, for_two = after(for_one, earlier), after(for_two, earlier)
    one = jnp.concatenate([one[:cut], add_low(one[cut:], for_one)])
    two = jnp.concatenate([add_low(two[:cut], for_two), two[cut:]])
    one_got, two_got = swap(one, axis, 1), swap(two, axis, 2)
    return own.astype(f32) + one_got.astype(f32) + two_got.astype(f32), two


def in_order(parts, rank):
    rows = parts[0].shape[0]
    whole = jnp.zeros((len(parts) * rows,) + parts[0].shape[1:], parts[0].dtype)
    for e, part in enumerate(parts):
        whole = lax.dynamic_update_slice_in_dim(whole, part, (rank ^ e) * rows, 0)
    return whole


def block_of(x, number, rows):
    return lax.dynamic_slice_in_dim(x, number * rows, rows, 0)


def both_cores(own, other, core):
    first = core == 0
    return jnp.concatenate([jnp.where(first, own, other), jnp.where(first, other, own)])


def sum_over_all(x):
    for axis in ("dp", "head", "mlp"):
        count = lax.axis_size(axis)
        if count == 4:
            x = (x + swap(x, axis, 1)) + (swap(x, axis, 2) + swap(x, axis, 3))
        else:
            mask = 1
            while mask < count:
                x = x + swap(x, axis, mask)
                mask *= 2
    return x


def rms_scale(rows):
    return lax.rsqrt(jnp.mean(rows * rows, axis=-1, keepdims=True) + epsilon)


def norm_back(rows, scale, gain, grad):
    weighted = grad * gain
    return scale * weighted - rows * scale * scale * scale * jnp.mean(
        weighted * rows, axis=-1, keepdims=True
    )


def turned(x, cosine, sine):
    half = HEAD_DIM // 2
    if x.shape[1] == HEAD_DIM:
        other = jnp.concatenate([x[:, half:], x[:, :half]], axis=1)
    else:
        lanes = x.shape[1]
        lane = lax.broadcasted_iota(jnp.int32, x.shape, 1)
        other = jnp.where(
            lane % HEAD_DIM < half, pltpu.roll(x, lanes - half, 1), pltpu.roll(x, half, 1)
        )
    return x * cosine + other * sine


def load_rows(refs, counts, number, target):
    at = 0
    for k, pieces in enumerate(counts):
        mine = refs[at : at + pieces]
        at += pieces

        @pl.when(number == k)
        def _(mine=mine):
            row = 0
            for ref in mine:
                target[row : row + ref.shape[0], :] = ref[...]
                row += ref.shape[0]


def project_kernel(counts, rank_ref, *refs):
    total = sum(counts)
    parts, (w_ref, gain_ref, cos_ref, sin_ref, first_ref) = refs[:total], refs[total : total + 5]
    a_ref, q_ref, k_ref, v_ref, norm_ref, rows_ref = refs[total + 5 :]
    e = pl.program_id(0)
    load_rows(parts, counts, e, rows_ref)
    x = rows_ref[...].astype(f32)
    a = (x * rms_scale(x) * gain_ref[...]).astype(bf16)
    a_ref[...] = a
    width = q_ref.shape[1]
    lanes = cos_ref.shape[1]
    cosine, sine = cos_ref[...], sin_ref[...]
    joined = dot(a, w_ref[...], NN)
    for g in range(width // lanes):
        at = slice(g * lanes, (g + 1) * lanes)
        q_ref[:, at] = turned(joined[:, at], cosine, sine).astype(bf16)
        at_k = slice(width + g * lanes, width + (g + 1) * lanes)
        k_ref[:, at] = turned(joined[:, at_k], cosine, sine).astype(bf16)
    first = first_ref[...].astype(f32)
    blended = blend_weight * joined[:, 2 * width :] + (1.0 - blend_weight) * first
    v_ref[...] = blended.astype(bf16)
    of = lax.broadcasted_iota(jnp.int32, (width, 128), 0) // HEAD_DIM
    one_hot = (of == lax.broadcasted_iota(jnp.int32, (width, 128), 1)).astype(f32)

    def norms(value):
        squares = lax.dot_general(
            value * value, one_hot, NN, precision=lax.Precision.HIGHEST, preferred_element_type=f32
        )
        return jnp.sum(jnp.sqrt(jnp.maximum(squares, 0.0)), axis=0, keepdims=True)

    @pl.when(e == 0)
    def _():
        norm_ref[...] = jnp.zeros_like(norm_ref)

    norm_ref[0:1, :] += norms(first)
    norm_ref[1:2, :] += norms(blended)


def spec_whole(x):
    return pl.BlockSpec(x.shape, lambda *_: (0,) * x.ndim)


def cost(us):
    return pl.CostEstimate(flops=int(us * 9e8), bytes_accessed=int(us * 1e5), transcendentals=0)


big = pltpu.CompilerParams(vmem_limit_bytes=56 * 1024 * 1024)


def project(rank, parts, weights, gain, cosine, sine, firsts):
    counts = tuple(len(p) for p in parts)
    flat = [x for p in parts for x in p]
    ranks, chunk = len(parts), parts[0][0].shape[0]
    length, width = firsts.shape
    model, lanes = flat[0].shape[1], cosine.shape[1]
    there = lambda e, r: (r[0] ^ e, 0)
    block = lambda n: pl.BlockSpec((chunk, n), there)
    spec = pltpu.PrefetchScalarGridSpec(
        num_scalar_prefetch=1,
        grid=(ranks,),
        in_specs=[spec_whole(x) for x in flat]
        + [spec_whole(weights), spec_whole(gain), block(lanes), block(lanes), block(width)],
        out_specs=[block(model), block(width), block(width), block(width)]
        + [pl.BlockSpec((8, 128), lambda e, r: (0, 0))],
        scratch_shapes=[pltpu.VMEM((chunk, model), bf16)],
    )
    low = jax.ShapeDtypeStruct((length, width), bf16)
    return pl.pallas_call(
        functools.partial(project_kernel, counts),
        grid_spec=spec,
        out_shape=[jax.ShapeDtypeStruct((length, model), bf16), low, low, low]
        + [jax.ShapeDtypeStruct((8, 128), f32)],
        compiler_params=big,
        cost_estimate=cost(9),
        name="project",
    )(rank[None], *flat, weights, gain, cosine, sine, firsts)


def feed_kernel(x_ref, g_ref, *refs):
    sources, (act_ref, in_ref, sum_ref) = (refs[0:3], refs[3:6], refs[6:9]), refs[-3:]
    f = pl.program_id(0)
    steps = pl.num_programs(0)

    @pl.when(f == 0)
    def _():
        sum_ref[...] = jnp.zeros_like(sum_ref)

    def work(gate_w, up_w, down_w):
        x, g = x_ref[...], g_ref[...]
        gate, up = dot(gate_w[...], x, NT), dot(up_w[...], x, NT)
        hidden_grad = dot(down_w[...], g, NT)
        sigma = 1.0 / (1.0 + jnp.exp(-gate))
        gate_sigma = gate * sigma
        hidden = (gate_sigma * up).astype(bf16)
        gate_grad = (hidden_grad * up * (sigma + gate_sigma * (1.0 - sigma))).astype(bf16)
        up_grad = (hidden_grad * gate_sigma).astype(bf16)
        act_ref[0, 0], act_ref[0, 1], act_ref[0, 2] = gate_grad, up_grad, hidden
        sum_ref[...] += dot(gate_grad, gate_w[...], TN) + dot(up_grad, up_w[...], TN)

    for k, condition in enumerate((f < 2, f == 2, f == 3)):

        @pl.when(condition)
        def _(k=k):
            work(*sources[k])

    @pl.when(f == steps - 1)
    def _():
        in_ref[...] = sum_ref[...].astype(in_ref.dtype)


def feed(x, grad, own, far, far_other, dtype, earlier=()):
    tokens, model = x.shape
    part = own.shape[0] // 6
    block = lambda at: pl.BlockSpec((part, model), at)
    return pl.pallas_call(
        feed_kernel,
        grid=(4,),
        in_specs=[spec_whole(x), spec_whole(grad)]
        + [block(lambda f, a=a: (2 * a + jnp.minimum(f, 1), 0)) for a in range(3)]
        + [block(lambda f, a=a: (a, 0)) for a in range(3)] * 2
        + [everywhere] * len(earlier),
        out_specs=[
            pl.BlockSpec((1, 3, part, tokens), lambda f: (f, 0, 0, 0)),
            pl.BlockSpec((tokens, model), lambda f: (0, 0)),
        ],
        out_shape=[
            jax.ShapeDtypeStruct((4, 3, part, tokens), bf16),
            jax.ShapeDtypeStruct((tokens, model), dtype),
        ],
        scratch_shapes=[pltpu.VMEM((tokens, model), f32)],
        compiler_params=big,
        cost_estimate=cost(14),
        name="feed",
    )(x, grad, *([own] * 3), *([far] * 3), *([far_other] * 3), *earlier)


def half_grads(act_ref, near_ref, x_ref, xn_ref, g_ref, gn_ref, result_ref):
    a = pl.program_id(0)

    @pl.when(a < 2)
    def _():
        result_ref[...] = dot(act_ref[0, 0], x_ref[...], NN) + dot(near_ref[0, 0], xn_ref[...], NN)

    @pl.when(a == 2)
    def _():
        result_ref[...] = dot(act_ref[0, 0], g_ref[...], NN) + dot(near_ref[0, 0], gn_ref[...], NN)


def other_grads_kernel(scalars, *refs):
    out_ref, result_ref = refs[-2:]
    half_grads(*refs[:6], result_ref)
    out_ref[...] = result_ref[...].astype(bf16)


def far_grads_kernel(ranks, scalars, *refs):
    got_ref, out_refs, result_ref = refs[6], refs[7 : 7 + ranks], refs[-1]
    half_grads(*refs[:6], result_ref)
    rows = result_ref.shape[0] // ranks
    for e in range(ranks):
        at = slice(e * rows, (e + 1) * rows)
        out_refs[e][0] = (result_ref[at, :] + got_ref[at, :].astype(f32)).astype(bf16)


def own_grads_kernel(ranks, scalars, *refs):
    got_ref, out_ref, out_got_ref = refs[6:9]
    own_refs, result_ref = refs[9 : 9 + ranks], refs[-1]
    half_grads(*refs[:6], result_ref)
    i = pl.program_id(0)
    rows = result_ref.shape[0] // ranks
    result_ref[...] += got_ref[...].astype(f32)

    @pl.when(i == 0)
    def _():
        for e in range(ranks):
            number = scalars[1] ^ e
            both = out_ref[number].astype(f32) + out_got_ref[number].astype(f32)
            own_refs[e][3 * rows :, :] = both.astype(bf16)

    for a in range(3):

        @pl.when(i == a)
        def _(a=a):
            to = slice(a * rows, (a + 1) * rows)
            for e in range(ranks):
                if rows % 8 == 0:
                    at = pl.ds(pl.multiple_of((scalars[1] ^ e) * rows, 8), rows)
                    own_refs[e][to, :] = result_ref[at, :].astype(bf16)
                else:
                    for h in range(ranks):

                        @pl.when(scalars[1] ^ e == h)
                        def _(e=e, h=h):
                            own_refs[e][to, :] = result_ref[h * rows : (h + 1) * rows, :].astype(bf16)


def shard_grads(scalars, ranks, far, here, near, x, x_near, grad, grad_near, got=None):
    _, _, part, tokens = here.shape
    model = x.shape[1]
    if got is None:
        number = lambda c: 3 if far else 1 - c[0]
    else:
        number = lambda c: 2 if far else c[0]
    act = pl.BlockSpec((1, 1, part, tokens), lambda i, c: (number(c), i, 0, 0))
    in_specs = [act, act] + [spec_whole(x)] * 4
    args = [here, near, x, x_near, grad, grad_near]
    row_block = pl.BlockSpec((part, model), lambda i, c: (i, 0))
    rows = part // ranks
    if got is None:
        kernel, out_specs = other_grads_kernel, row_block
        out_shape = jax.ShapeDtypeStruct((3 * part, model), bf16)
    elif far:
        kernel = functools.partial(far_grads_kernel, ranks)
        in_specs.append(row_block)
        args += got
        out_specs = [pl.BlockSpec((1, rows, model), lambda i, c: (i, 0, 0))] * ranks
        out_shape = [jax.ShapeDtypeStruct((3, rows, model), bf16)] * ranks
    else:
        kernel = functools.partial(own_grads_kernel, ranks)
        in_specs += [row_block] + [spec_whole(g) for g in got[1:]]
        args += got
        wide = 3 * rows + got[1].shape[1]
        out_specs = [pl.BlockSpec((wide, model), lambda i, c: (0, 0))] * ranks
        out_shape = [jax.ShapeDtypeStruct((wide, model), bf16)] * ranks
    spec = pltpu.PrefetchScalarGridSpec(
        num_scalar_prefetch=1,
        grid=(3,),
        in_specs=in_specs,
        out_specs=out_specs,
        scratch_shapes=[pltpu.VMEM((part, model), f32)],
    )
    return pl.pallas_call(
        kernel,
        grid_spec=spec,
        out_shape=out_shape,
        compiler_params=big,
        cost_estimate=cost(6),
        name=("far" if far else "own") + ("_other" if got is None else "_sum"),
    )(scalars, *args)


def down_kernel(here_ref, near_ref, own_ref, far_ref, other_ref, out_ref, out_near_ref, sum_ref):
    f = pl.program_id(0)
    steps = pl.num_programs(0)

    @pl.when(f == 0)
    def _():
        sum_ref[...] = jnp.zeros_like(sum_ref)

    for condition, ref in ((f < 2, own_ref), (f == 2, far_ref), (f == 3, other_ref)):

        @pl.when(condition)
        def _(ref=ref):
            sum_ref[0] += dot(here_ref[0, 0], ref[...], TN)
            sum_ref[1] += dot(near_ref[0, 0], ref[...], TN)

    @pl.when(f == steps - 1)
    def _():
        out_ref[...] = sum_ref[0]
        out_near_ref[...] = sum_ref[1].astype(bf16)


def down(here, near, own, far, far_other):
    steps, _, part, tokens = here.shape
    model = own.shape[1]
    act = pl.BlockSpec((1, 1, part, tokens), lambda f: (f, 2, 0, 0))
    return pl.pallas_call(
        down_kernel,
        grid=(steps,),
        in_specs=[act, act]
        + [pl.BlockSpec((part, model), lambda f: (4 + jnp.minimum(f, 1), 0))]
        + [pl.BlockSpec((part, model), lambda f: (2, 0))] * 2,
        out_specs=[pl.BlockSpec((tokens, model), lambda f: (0, 0))] * 2,
        out_shape=[
            jax.ShapeDtypeStruct((tokens, model), f32),
            jax.ShapeDtypeStruct((tokens, model), bf16),
        ],
        scratch_shapes=[pltpu.VMEM((2, tokens, model), f32)],
        compiler_params=big,
        cost_estimate=cost(8),
        name="down",
    )(here, near, own, far, far_other)


def unproject_kernel(counts, groups, rank_ref, *refs):
    total = sum(counts)
    parts = refs[:total]
    w_ref, cos_ref, sin_ref = refs[total : total + 3]
    grads = refs[total + 3 : total + 3 + 3 * groups]
    p_ref, first_ref, g_ref, gain_ref, rows_ref = refs[-5:]
    e = pl.program_id(0)
    load_rows(parts, counts, e, rows_ref)
    x = rows_ref[...].astype(f32)
    width, lanes = first_ref.shape[1], cos_ref.shape[1]
    cosine, sine = cos_ref[...], -sin_ref[...]
    for g in range(groups):
        dq_ref, dk_ref, dv_ref = grads[3 * g : 3 * g + 3]
        at = slice(g * lanes, (g + 1) * lanes)
        at_k = slice(width + g * lanes, width + (g + 1) * lanes)
        at_v = slice(2 * width + g * lanes, 2 * width + (g + 1) * lanes)
        p_ref[:, at] = turned(dq_ref[...], cosine, sine).astype(bf16)
        p_ref[:, at_k] = turned(dk_ref[...], cosine, sine).astype(bf16)
        blend = dv_ref[...].astype(bf16).astype(f32)
        p_ref[:, at_v] = (blend_weight * blend).astype(bf16)
        first_ref[:, at] = ((1.0 - blend_weight) * blend).astype(bf16)
    grad = dot(p_ref[...], w_ref[...], NT)
    g_ref[0] = grad.astype(bf16)

    @pl.when(e == 0)
    def _():
        gain_ref[...] = jnp.zeros_like(gain_ref)

    gain_ref[...] += jnp.sum(grad * (x * rms_scale(x)), axis=0, keepdims=True)


def unproject(rank, parts, weights, cosine, sine, grads, earlier):
    counts = tuple(len(p) for p in parts)
    flat = [x for p in parts for x in p]
    ranks, chunk = len(parts), parts[0][0].shape[0]
    length, lanes = grads[0].shape
    groups = len(grads) // 3
    width, model = groups * lanes, flat[0].shape[1]
    there = lambda e, r: (r[0] ^ e, 0)
    block = lambda n: pl.BlockSpec((chunk, n), there)
    spec = pltpu.PrefetchScalarGridSpec(
        num_scalar_prefetch=1,
        grid=(ranks,),
        in_specs=[spec_whole(x) for x in flat]
        + [spec_whole(weights), block(lanes), block(lanes)]
        + [block(lanes)] * (3 * groups)
        + [everywhere] * len(earlier),
        out_specs=[
            block(3 * width),
            block(width),
            pl.BlockSpec((1, chunk, model), lambda e, r: (e, 0, 0)),
            pl.BlockSpec((1, model), lambda e, r: (0, 0)),
        ],
        scratch_shapes=[pltpu.VMEM((chunk, model), bf16)],
    )
    return pl.pallas_call(
        functools.partial(unproject_kernel, counts, groups),
        grid_spec=spec,
        out_shape=[
            jax.ShapeDtypeStruct((length, 3 * width), bf16),
            jax.ShapeDtypeStruct((length, width), bf16),
            jax.ShapeDtypeStruct((ranks, chunk, model), bf16),
            jax.ShapeDtypeStruct((1, model), f32),
        ],
        compiler_params=big,
        cost_estimate=cost(12),
        name="unproject",
    )(rank[None], *flat, weights, cosine, sine, *grads, *earlier)


def on_device(
    tokens,
    first_values,
    segment_ids,
    positions,
    attn_gain,
    w_query,
    w_key,
    w_value,
    w_out,
    mlp_gain,
    w_gate,
    w_up,
    w_down,
    out_grad,
):
    core, rank = lax.axis_index("dp"), lax.axis_index("head")
    ranks = lax.axis_size("head")
    chunk, width = tokens.shape[0], w_query.shape[1]
    model = tokens.shape[2]
    length, ff = segment_ids.shape[0], w_gate.shape[1]
    block = min(512, length)
    tokens, firsts, out_grad = tokens[:, 0], first_values[:, 0], out_grad[:, 0]
    places = positions[:, 0]
    start = jnp.arange(length, dtype=jnp.int32) - places

    row_parts = spread_relay(tokens, "head")

    part = ff // 2
    rows = part // ranks
    stack = jnp.concatenate([w_gate.T, w_up.T, w_down])
    cut_stack = stack.reshape(3, 2 * ranks, rows, model)
    far_piece = swap(
        lax.dynamic_index_in_dim(cut_stack, core * ranks + rank, 1, False), "mlp", 2
    ).reshape(3 * rows, model)
    out_grad_near = swap(out_grad, "mlp", 1)
    half_out = width // 2
    bundle = jnp.concatenate([far_piece, block_of(w_out, core, half_out)])
    bundle = after(bundle, *row_parts[-1])
    bundles = spread(bundle, "head")

    w_project = jnp.concatenate([w_query, w_key, w_value], axis=1)
    lanes = min(128, width)
    lane = jnp.arange(lanes)
    freq = theta_base ** (-(lane % (HEAD_DIM // 2)).astype(f32) * 2.0 / HEAD_DIM)
    angles = places.astype(f32)[:, None] * freq
    cosine = jnp.cos(angles)
    sine = jnp.sin(angles) * jnp.where(lane % HEAD_DIM < HEAD_DIM // 2, -1.0, 1.0)
    gathered, queries, keys, values, norms = project(
        rank, row_parts, w_project, attn_gain[None], cosine, sine, firsts
    )
    mixed, log_total = attend_forward2(queries, keys, values, start, block)

    mixed_here = lax.all_to_all(mixed, "head", 0, 0, tiled=True).reshape(ranks, chunk, width)

    bundles = [bundles[0]] + [after(b, mixed) for b in bundles[1:]]
    far_half = jnp.stack([b[: 3 * rows].reshape(3, rows, model) for b in bundles], axis=1)
    far_half = far_half.reshape(3 * part, model)
    out_half = in_order([b[3 * rows :] for b in bundles], rank).reshape(ranks, half_out, model)
    far_other, out_other = swap(far_half, "dp", 1), swap(out_half, "dp", 1)
    first = core == 0
    out_all = jnp.concatenate(
        [jnp.where(first, out_half, out_other), jnp.where(first, out_other, out_half)], axis=1
    )

    residual = tokens.astype(f32)
    hidden_state = residual + jnp.einsum("htk,hkd->td", mixed_here, out_all, preferred_element_type=f32)
    mlp_scale = rms_scale(hidden_state)
    mlp_input = (hidden_state * mlp_scale * mlp_gain).astype(bf16)
    mlp_input_near = swap(mlp_input, "mlp", 1)

    acts, terms = feed(mlp_input, out_grad, stack, far_half, far_other, f32)
    acts_near, terms_near = feed(
        mlp_input_near, out_grad_near, stack, far_half, far_other, bf16, (terms,)
    )
    terms_back = swap(terms_near, "mlp", 1)
    scalars = jnp.stack([core, rank]).astype(jnp.int32)
    tokens_two = (acts, acts_near, mlp_input, mlp_input_near, out_grad, out_grad_near)
    far_other_grads = shard_grads(scalars, ranks, True, *tokens_two)
    own_other_grads = shard_grads(scalars, ranks, False, *tokens_two)
    far_half_got = swap(far_other_grads, "dp", 1)
    own_half_got = swap(after(own_other_grads, far_half_got), "dp", 1)
    down_here, down_near = down(acts, acts_near, stack, far_half, far_other)

    far_chip = shard_grads(scalars, ranks, True, *tokens_two, [far_half_got])
    far_got = [swap(f, "head", e) for e, f in enumerate(far_chip) if e]
    mlp_normed_grad = after(terms_back, down_near, far_chip[0]).astype(f32) + terms
    mlp_gain_grad = jnp.sum(mlp_normed_grad * hidden_state * mlp_scale, axis=0)
    state_grad = out_grad.astype(f32) + norm_back(hidden_state, mlp_scale, mlp_gain, mlp_normed_grad)
    state_grad_low = state_grad.astype(bf16)

    mixed_grad = jnp.einsum(
        "td,hkd->htk", state_grad_low, out_all, preferred_element_type=f32
    ).astype(bf16)
    mixed_grad_rows = lax.all_to_all(mixed_grad, "head", 0, 0, tiled=True).reshape(length, width)

    out_grads = jnp.einsum(
        "htk,td->hkd", mixed_here, state_grad_low, preferred_element_type=f32
    ).astype(bf16).reshape(ranks, 2, half_out, model)
    out_got = swap(lax.dynamic_index_in_dim(out_grads, 1 - core, 1, False), "dp", 1)
    out_own = lax.dynamic_index_in_dim(out_grads, core, 1, False)
    far_sum = add_low(far_chip[0], *far_got)
    own_half_got = after(own_half_got, mixed_grad, far_sum)
    own_chip = shard_grads(scalars, ranks, False, *tokens_two, [own_half_got, out_own, out_got])
    mixed_grad_rows = after(mixed_grad_rows, own_chip[0])
    down_back = swap(after(down_near, mixed_grad_rows), "mlp", 1)
    output = (hidden_state + down_back.astype(f32) + down_here).astype(bf16)

    far_here = swap(far_sum, "mlp", 2)
    own_chip = [own_chip[0]] + [after(f, mixed_grad_rows) for f in own_chip[1:]]
    own_got = [swap(f, "head", e) for e, f in enumerate(own_chip) if e]
    grads = []
    earlier = (far_sum, *own_chip[1:])
    for g in range(width // lanes):
        grads += attend_backward(
            queries, keys, values, mixed_grad_rows, mixed, log_total, start, block, g, earlier
        )
        earlier = (grads[-1],)
    own_sum = sum(f.astype(f32) for f in (own_chip[0], *own_got))
    piece_sum = add_low(own_sum[: 3 * rows].reshape(3, rows, model), far_here)
    out_sum = own_sum[3 * rows :].astype(bf16)

    proj_grad, first_values_grad, normed, attn_gain_grad = unproject(
        rank, row_parts, w_project, cosine, sine, grads, (piece_sum,)
    )
    pieces = spread(piece_sum, "head")
    half_sum = jnp.zeros((3, ranks, rows, model), bf16)
    for e, piece in enumerate(pieces):
        half_sum = lax.dynamic_update_slice_in_dim(half_sum, piece[:, None], rank ^ e, 1)
    half_sum = half_sum.reshape(3, part, model)
    other_sum = swap(half_sum, "dp", 1)
    ff_grads = jnp.concatenate(
        [jnp.where(first, half_sum, other_sum), jnp.where(first, other_sum, half_sum)], axis=1
    ).astype(f32)
    gate_wgrad, up_wgrad, down_wgrad = ff_grads[0].T, ff_grads[1].T, ff_grads[2]

    proj_wgrad = dot(gathered, proj_grad, TN).astype(bf16)
    half_proj = model // 2
    proj_mine = add_low(
        block_of(proj_wgrad, core, half_proj),
        swap(block_of(proj_wgrad, 1 - core, half_proj), "dp", 1),
    )
    attn_normed_grad, last = collect_relay([normed[e] for e in range(ranks)], "head", proj_mine)
    input_grad = (
        state_grad + norm_back(residual, rms_scale(residual), attn_gain, attn_normed_grad)
    ).astype(bf16)
    line, count = lax.axis_index("mlp"), lax.axis_size("mlp")

    def over_line(x):
        part = x.shape[0] // count
        piece = collect([block_of(x, line ^ e, part) for e in range(count)], "mlp").astype(bf16)
        got = spread(piece, "mlp")
        return in_order(got, line), got[-1]

    proj_half, proj_last = over_line(proj_mine)
    proj_sum = both_cores(proj_half, swap(proj_half, "dp", 1), core).astype(f32)
    out_half_sum, _ = over_line(after(out_sum, proj_last))
    out_wgrad = both_cores(out_half_sum, swap(out_half_sum, "dp", 1), core).astype(f32)

    norm_row = jnp.zeros((model,), f32).at[:2].set(jnp.sum(norms[:2], axis=1))
    small = sum_over_all(after(jnp.stack([attn_gain_grad[0], mlp_gain_grad, norm_row]), proj_last))
    devices = lax.axis_size("dp") * ranks * count
    value_norms = small[2, :2] / (length * (width // HEAD_DIM) * devices)
    return (
        output[:, None],
        input_grad[:, None],
        first_values_grad[:, None],
        small[0],
        proj_sum[:, :width],
        proj_sum[:, width : 2 * width],
        proj_sum[:, 2 * width :],
        out_wgrad,
        small[1],
        gate_wgrad,
        up_wgrad,
        down_wgrad,
        value_norms,
    )


def solution(mesh):
    placed = (
        P("head", ("dp", "mlp"), None),
        P(None, ("dp", "mlp"), "head"),
        P(None, ("dp", "mlp")),
        P(None, ("dp", "mlp")),
        P(),
        P(None, "head"),
        P(None, "head"),
        P(None, "head"),
        P("head", None),
        P(),
        P(None, "mlp"),
        P(None, "mlp"),
        P("mlp", None),
        P("head", ("dp", "mlp"), None),
    )
    return jax.shard_map(
        on_device,
        mesh=mesh,
        in_specs=placed,
        out_specs=(
            P("head", ("dp", "mlp"), None),
            P("head", ("dp", "mlp"), None),
            P(None, ("dp", "mlp"), "head"),
            P(),
            P(None, "head"),
            P(None, "head"),
            P(None, "head"),
            P("head", None),
            P(),
            P(None, "mlp"),
            P(None, "mlp"),
            P("mlp", None),
            P(),
        ),
        check_vma=False,
    )
```

time: 847 us -> 452 us (0.53)
  waiting for transfers between devices: 517 us -> 104 us
  Pallas kernels: 69.1 us -> 174 us
  matrix products: 84.8 us -> 14.3 us
  starting transfers between devices: 1.4 us -> 61.4 us
  blocking collectives: 45 us -> 0 us
  between operations: 14.8 us -> 2.11 us
  local copies, waits for them, and re-layouts: 50.2 us -> 40.8 us
  other arithmetic: 55.7 us -> 46.6 us
    reduce_scatter x4 -> x0, waiting for transfers between devices: 237 us -> none  [the longest x1 83.7 us: on_device(): lax.psum_scatter(jnp.einsum('lrh,hd->lrd', part, w_out, preferred_element...]
    all_gather x4 -> x0, waiting for transfers between devices: 228 us -> none  [the longest x1 74.8 us: on_device(): piece = lax.all_gather(mlp_input, 'mlp', axis=1, tiled=True)]
    pallas_call x0 -> x25, Pallas kernels: none -> 103 us  [the longest x2 32.8 us: feed(): pl.pallas_call(feed_kernel, grid=(4,), in_specs=[spec_whole(x), spec_whol...]
    ppermute x0 -> x54, waiting for transfers between devices: none -> 92.9 us  [swap(): lax.ppermute(x, axis, [(i, i ^ mask) for i in range(lax.axis_size(axis))])]
    dot_general x12 -> x4, matrix products: 84.8 us -> 14.3 us  [the longest x1 5.69 us: dot(): return lax.dot_general(a, b, dims, preferred_element_type=jnp.float32)]
    ppermute x0 -> x54, starting transfers between devices: none -> 53.5 us  [swap(): lax.ppermute(x, axis, [(i, i ^ mask) for i in range(lax.axis_size(axis))])]
    psum x2 -> x0, waiting for transfers between devices: 51.8 us -> none  [the longest x1 51.7 us: on_device(): lax.psum(proj_wgrad[:, :width].astype(jnp.bfloat16), ('dp', 'mlp'))]
    psum x1 -> x0, blocking collectives: 45 us -> none  [on_device(): lax.psum((attn_gain_grad, mlp_gain_grad, norm_local), ('dp', 'head', 'mlp'))]
  transfers between devices with their start and end apart: 10 -> 56, of which waited for: 9 -> 24; matrix products, arithmetic and copies ran while one was open for 13% -> 17% of each run, Pallas kernels for 5% -> 34%
where the time goes in v2:
time: 452 us; the launch traced here: 443 us
  Pallas kernels  174 us (38%)
  waiting for transfers between devices  104 us (23%)
  starting transfers between devices  61.4 us (14%)
  other arithmetic  46.6 us (10%)
  local copies, waits for them, and re-layouts  40.8 us (9%)
  matrix products  14.3 us (3%)
    ppermute x54, waiting for transfers between devices, swap(): lax.ppermute(x, axis, [(i, i ^ mask) for i in range(lax.axis_size(axis))])  92.9 us
    ppermute x54, starting transfers between devices, swap(): lax.ppermute(x, axis, [(i, i ^ mask) for i in range(lax.axis_size(axis))])  53.5 us
    pallas_call x2, Pallas kernels, attend_backward(): pl.pallas_call(functools.partial(backward_kernel, block), grid_spec=spec,...  44.4 us
    pallas_call x2, Pallas kernels, feed(): pl.pallas_call(feed_kernel, grid=(4,), in_specs=[spec_whole(x), spec_whol...  32.8 us
    pallas_call x4, Pallas kernels, shard_grads(): pl.pallas_call(kernel, grid_spec=spec, out_shape=out_shape, compiler_para...  32.4 us
    pallas_call x1, Pallas kernels, attend_forward2(): pl.pallas_call(functools.partial(fwd2_kernel, block), grid_spec=spec, out...  27.5 us
    pallas_call x1, Pallas kernels, project(): pl.pallas_call(functools.partial(project_kernel, counts), grid_spec=spec,...  14.1 us
    pallas_call x1, Pallas kernels, unproject(): pl.pallas_call(functools.partial(unproject_kernel, counts, groups), grid_...  14 us
  transfers between devices with their start and end apart: 56, of which 24 were waited for; matrix products, arithmetic and copies ran while one was open for 17% of the time, Pallas kernels for 34%

profile of v2, /device:TPU:0, one launch (start us, length us, event | category | flops | bytes accessed | tf_op | source)
XLA Modules:
  0.0 443.3 jit_solution(556092049506295368)
XLA Ops:
  0.7 3.0 collective-permute-start
  5.2 2.6 pad_maximum_fusion.refs_0_.refs_1_.refs_2_.own_ref
  7.9 2.7 collective-permute-start.4
  10.9 5.6 %fusion.11 = (f32[2048,128]{1,0:T(8,128)}, f32[2048,128]{1,0:T(8,128)}) fusion(f32[128]{0:T(128)S(1)} %get-tuple-element.133, f32[128]{0:T(128)S(1)} %get-tuple-element.134, f32[2048]{0:T(1024)S(1)} %bitcast.133), kind=kLoop, calls=%fused_computation.42 | loop fusion | flops 524288 | bytes 2106368 | tf_op jit(solution)/shard_map/mul | solution.py:697
  16.5 12.1 %collective-permute-done.1.refs_2_ = bf16[512,1024]{1,0:T(8,128)(2,1)} collective-permute-done((bf16[512,1024]{1,0:T(8,128)(2,1)}, bf16[512,1024]{1,0:T(8,128)(2,1)}, u32[]{:S(2)}, u32[]{:S(2)}) %collective-permute-start.1) | collective-permute-done | bytes 1048608 | tf_op jit(solution)/shard_map/ppermute | solution.py:172
  34.8 7.4 %collective-permute-done.2.refs_3_.refs_1_ = bf16[256,1024]{1,0:T(8,128)(2,1)S(1)} collective-permute-done((bf16[256,1024]{1,0:T(8,128)(2,1)S(1)}, bf16[256,1024]{1,0:T(8,128)(2,1)S(1)}, u32[]{:S(2)}, u32[]{:S(2)}) %collective-permute-start.2) | collective-permute-done | bytes 524320 | tf_op jit(solution)/shard_map/ppermute | solution.py:172
  48.1 14.1 %project.1 = (bf16[2048,1024]{1,0:T(8,128)(2,1)}, bf16[2048,256]{1,0:T(8,128)(2,1)}, bf16[2048,256]{1,0:T(8,128)(2,1)}, bf16[2048,256]{1,0:T(8,128)(2,1)}, f32[8,128]{1,0:T(8,128)}) custom-call(s32[1]{0:T(128)} %bitcast.2.rank_ref, bf16[512,1024]{1,0:T(8,128)(2,1)} %bitcast.122, bf16[512,1024]{1,0:T(8,128)(2,1)} %collective-permute-done.refs_1_, ...), custom_call_target="tpu_custom_call" | custom-call | flops 8099999744 | bytes 900000 | tf_op jit(solution)/shard_map/project/pallas_call | solution.py:364
  65.9 27.5 %attend_forward.1 = (bf16[2048,256]{1,0:T(8,128)(2,1)}, f32[2,8,2048]{2,1,0:T(8,128)S(1)}) custom-call(s32[4]{0:T(128)S(1)} %slice.130.firsts, s32[4]{0:T(128)S(1)} %slice.131.lasts, bf16[2048,256]{1,0:T(8,128)(2,1)S(1)} %copy-done.5, bf16[2048,256]{1,0:T(8,128)(2,1)S(1)} %copy-done.7, bf16[2048,256]{1,0:T(8,128)(2,1)S(1)} %copy-done.9, ...), custom_call_target="tpu_custom_call" | custom-call | flops 25769803776 | bytes 4194304 | tf_op jit(solution)/shard_map/attend_forward/pallas_call | solution.py:88
  106.3 3.7 all-to-all-start
  110.7 2.7 broadcast_select_fusion.3
  113.4 10.6 %all-to-all-done = bf16[4,512,256]{2,1,0:T(8,128)(2,1)S(1)} async-done(((bf16[4,512,256]{2,1,0:T(8,128)(2,1)}), bf16[4,512,256]{2,1,0:T(8,128)(2,1)S(1)}, u32[]{:S(2)}, u32[]{:S(2)}) %all-to-all-start) | async-done | bytes 1048608 | tf_op jit(solution)/shard_map/all_to_all | solution.py:703
  125.0 3.5 multiply_reduce_fusion.2
  130.1 16.4 %feed.2 = (bf16[4,3,352,512]{3,2,1,0:T(8,128)(2,1)}, f32[512,1024]{1,0:T(8,128)}) custom-call(bf16[512,1024]{1,0:T(8,128)(2,1)} %copy-done.38, bf16[512,1024]{1,0:T(8,128)(2,1)} %bitcast.15.g_ref.refs_4_, bf16[2112,1024]{1,0:T(8,128)(2,1)} %copy-done.24, bf16[2112,1024]{1,0:T(8,128)(2,1)} %copy-done.24, bf16[2112,1024]{1,0:T(8,128)(2,1)} %copy-done.24, ...), custom_call_target="tpu_custom_call" | custom-call | flops 12600000512 | bytes 1400000 | tf_op jit(solution)/shard_map/feed/pallas_call | solution.py:411
  146.5 11.3 %collective-permute-done.10.x_ref.refs_3_ = bf16[512,1024]{1,0:T(8,128)(2,1)S(1)} collective-permute-done((bf16[512,1024]{1,0:T(8,128)(2,1)S(1)}, bf16[512,1024]{1,0:T(8,128)(2,1)S(1)}, u32[]{:S(2)}, u32[]{:S(2)}) %collective-permute-start.10) | collective-permute-done | bytes 1048608 | tf_op jit(solution)/shard_map/ppermute | solution.py:172
  158.8 16.4 %feed.3 = (bf16[4,3,352,512]{3,2,1,0:T(8,128)(2,1)}, bf16[512,1024]{1,0:T(8,128)(2,1)}) custom-call(bf16[512,1024]{1,0:T(8,128)(2,1)} %copy-done.51, bf16[512,1024]{1,0:T(8,128)(2,1)} %collective-permute-done.11.g_ref.refs_5_, bf16[2112,1024]{1,0:T(8,128)(2,1)} %copy-done.24, bf16[2112,1024]{1,0:T(8,128)(2,1)} %copy-done.24, bf16[2112,1024]{1,0:T(8,128)(2,1)} %copy-done.24, ...), custom_call_target="tpu_custom_call" | custom-call | flops 12600000512 | bytes 1400000 | tf_op jit(solution)/shard_map/feed/pallas_call | solution.py:411
  175.2 7.3 %far_other.1 = bf16[1056,1024]{1,0:T(8,128)(2,1)} custom-call(s32[2]{0:T(128)} %pad_add_fusion.scalars, bf16[4,3,352,512]{3,2,1,0:T(8,128)(2,1)} %get-tuple-element.60.here_ref.refs_0_, bf16[4,3,352,512]{3,2,1,0:T(8,128)(2,1)} %get-tuple-element.62.near_ref.refs_1_, bf16[512,1024]{1,0:T(8,128)(2,1)} %copy-done.38, bf16[512,1024]{1,0:T(8,128)(2,1)} %copy-done.51, ...), custom_call_target="tpu_custom_call" | custom-call | flops 5400000000 | bytes 600000 | tf_op jit(solution)/shard_map/far_other/pallas_call | solution.py:527
  183.0 9.2 %down.1 = (f32[512,1024]{1,0:T(8,128)}, bf16[512,1024]{1,0:T(8,128)(2,1)}) custom-call(bf16[4,3,352,512]{3,2,1,0:T(8,128)(2,1)} %get-tuple-element.60.here_ref.refs_0_, bf16[4,3,352,512]{3,2,1,0:T(8,128)(2,1)} %get-tuple-element.62.near_ref.refs_1_, bf16[2112,1024]{1,0:T(8,128)(2,1)} %copy-done.24, ...), custom_call_target="tpu_custom_call" | custom-call | flops 7200000000 | bytes 800000 | tf_op jit(solution)/shard_map/down/pallas_call | solution.py:562
  192.2 7.7 %own_other.1.refs_0_ = bf16[1056,1024]{1,0:T(8,128)(2,1)} custom-call(s32[2]{0:T(128)} %pad_add_fusion.scalars, bf16[4,3,352,512]{3,2,1,0:T(8,128)(2,1)} %get-tuple-element.60.here_ref.refs_0_, bf16[4,3,352,512]{3,2,1,0:T(8,128)(2,1)} %get-tuple-element.62.near_ref.refs_1_, bf16[512,1024]{1,0:T(8,128)(2,1)} %copy-done.38, bf16[512,1024]{1,0:T(8,128)(2,1)} %copy-done.51, ...), custom_call_target="tpu_custom_call" | custom-call | flops 5400000000 | bytes 600000 | tf_op jit(solution)/shard_map/own_other/pallas_call | solution.py:527
  200.0 7.9 %far_sum.1 = (bf16[3,88,1024]{2,1,0:T(8,128)(2,1)}, bf16[3,88,1024]{2,1,0:T(8,128)(2,1)}, bf16[3,88,1024]{2,1,0:T(8,128)(2,1)}, bf16[3,88,1024]{2,1,0:T(8,128)(2,1)}) custom-call(s32[2]{0:T(128)} %pad_add_fusion.scalars, bf16[4,3,352,512]{3,2,1,0:T(8,128)(2,1)} %get-tuple-element.60.here_ref.refs_0_, ...), custom_call_target="tpu_custom_call" | custom-call | flops 5400000000 | bytes 600000 | tf_op jit(solution)/shard_map/far_sum/pallas_call | solution.py:527
  208.6 2.7 multiply_reduce_fusion
  211.4 3.1 subtract_add_fusion
  218.1 2.7 collective-permute-start.17
  222.5 3.8 fusion.10.refs_1_
  226.3 4.2 all-to-all-start.1
  230.5 3.9 collective-permute-done.17
  234.4 11.8 %collective-permute-done.16 = bf16[3,88,1024]{2,1,0:T(8,128)(2,1)} collective-permute-done((bf16[3,88,1024]{2,1,0:T(8,128)(2,1)}, bf16[3,88,1024]{2,1,0:T(8,128)(2,1)}, u32[]{:S(2)}, u32[]{:S(2)}) %collective-permute-start.16) | collective-permute-done | bytes 540704 | tf_op jit(solution)/shard_map/ppermute | solution.py:172
  246.4 2.4 add_convert_fusion.3.refs_2_.rest_0_
  248.8 9.5 %own_sum.1 = (bf16[392,1024]{1,0:T(8,128)(2,1)}, bf16[392,1024]{1,0:T(8,128)(2,1)}, bf16[392,1024]{1,0:T(8,128)(2,1)}, bf16[392,1024]{1,0:T(8,128)(2,1)}) custom-call(s32[2]{0:T(128)} %pad_add_fusion.scalars, bf16[4,3,352,512]{3,2,1,0:T(8,128)(2,1)} %get-tuple-element.60.here_ref.refs_0_, bf16[4,3,352,512]{3,2,1,0:T(8,128)(2,1)} %get-tuple-element.62.near_ref.refs_1_, ...), custom_call_target="tpu_custom_call" | custom-call | flops 5400000000 | bytes 600000 | tf_op jit(solution)/shard_map/own_sum/pallas_call | solution.py:527
  264.9 22.4 %attend_backward.2 = (f32[2048,128]{1,0:T(8,128)S(1)}, f32[2048,128]{1,0:T(8,128)S(1)}, f32[2048,128]{1,0:T(8,128)}) custom-call(s32[4]{0:T(128)S(1)} %get-tuple-element.130.full_end, s32[4]{0:T(128)S(1)} %get-tuple-element.129.some_end, bf16[2048,256]{1,0:T(8,128)(2,1)} %get-tuple-element.56.q_ref, bf16[2048,256]{1,0:T(8,128)(2,1)} %get-tuple-element.57.k_ref, ...), custom_call_target="tpu_custom_call" | custom-call | flops 19327352832 | bytes 5767168 | tf_op jit(solution)/shard_map/attend_backward/pallas_call | solution.py:159
  287.4 22.0 %attend_backward.3 = (f32[2048,128]{1,0:T(8,128)S(1)}, f32[2048,128]{1,0:T(8,128)S(1)}, f32[2048,128]{1,0:T(8,128)S(1)}) custom-call(s32[4]{0:T(128)S(1)} %get-tuple-element.130.full_end, s32[4]{0:T(128)S(1)} %get-tuple-element.129.some_end, bf16[2048,256]{1,0:T(8,128)(2,1)S(1)} %copy-done.6, bf16[2048,256]{1,0:T(8,128)(2,1)S(1)} %copy-done.8, ...), custom_call_target="tpu_custom_call" | custom-call | flops 19327352832 | bytes 5767168 | tf_op jit(solution)/shard_map/attend_backward/pallas_call | solution.py:159
  317.7 14.0 %unproject.1 = (bf16[2048,768]{1,0:T(8,128)(2,1)}, bf16[2048,256]{1,0:T(8,128)(2,1)}, bf16[4,512,1024]{2,1,0:T(8,128)(2,1)}, f32[1,1024]{1,0:T(1,128)}) custom-call(s32[1]{0:T(128)} %bitcast.2.rank_ref, bf16[512,1024]{1,0:T(8,128)(2,1)} %bitcast.123, bf16[512,1024]{1,0:T(8,128)(2,1)} %collective-permute-done.refs_1_, ...), custom_call_target="tpu_custom_call" | custom-call | flops 10800000000 | bytes 1200000 | tf_op jit(solution)/shard_map/unproject/pallas_call | solution.py:635
  331.7 2.8 slice_bitcast_fusion.6
  336.6 5.7 %convolution_convert_fusion.1 = bf16[1024,768]{1,0:T(8,128)(2,1)S(1)} fusion(bf16[2048,1024]{1,0:T(8,128)(2,1)S(1)} %copy-done.52, bf16[2048,768]{1,0:T(8,128)(2,1)} %get-tuple-element.83), kind=kOutput, calls=%fused_computation.32 | convolution fusion | flops 3222011904 | bytes 8912896 | tf_op jit(solution)/shard_map/dot_general | solution.py:18
  347.7 4.4 collective-permute-start.29
  352.1 6.6 %collective-permute-done.27.refs_0_ = bf16[256,1024]{1,0:T(8,128)(2,1)} collective-permute-done((bf16[256,1024]{1,0:T(8,128)(2,1)}, bf16[256,1024]{1,0:T(8,128)(2,1)}, u32[]{:S(2)}, u32[]{:S(2)}) %collective-permute-start.27) | collective-permute-done | bytes 524320 | tf_op jit(solution)/shard_map/ppermute | solution.py:172
  360.6 3.9 collective-permute-done.30
  372.0 2.3 collective-permute-start.41
  374.3 2.2 collective-permute-done.32.refs_1_
  377.6 3.9 collective-permute-done.40
  382.4 3.1 collective-permute-done.41
  390.8 3.8 collective-permute-done.35
  394.5 2.1 collective-permute-start.45
  396.7 2.3 collective-permute-start.43
  409.5 4.0 collective-permute-done.46
  414.5 4.8 %collective-permute-done.47 = bf16[32,1024]{1,0:T(8,128)(2,1)S(1)} collective-permute-done((bf16[32,1024]{1,0:T(8,128)(2,1)S(1)}, bf16[32,1024]{1,0:T(8,128)(2,1)S(1)}, u32[]{:S(2)}, u32[]{:S(2)}) %collective-permute-start.47) | collective-permute-done | bytes 65568 | tf_op jit(solution)/shard_map/ppermute | solution.py:172
  421.0 4.3 collective-permute-done.48
  430.9 3.2 fusion.17
  439.2 3.7 slice_bitcast_fusion
  (289 shorter events, 104.0 us)
Async XLA Ops:
  0.7 29.5 %collective-permute-start = (bf16[512,1024]{1,0:T(8,128)(2,1)}, bf16[512,1024]{1,0:T(8,128)(2,1)}, u32[]{:S(2)}, u32[]{:S(2)}) collective-permute-start(bf16[512,1024]{1,0:T(8,128)(2,1)} %bitcast.120), channel_id=1, source_target_pairs={{0,4},{4,0},{8,12},{12,8},{1,5},{5,1},{9,13},{13,9},{2,6},{6,2},{1... | collective-permute-start | bytes 3145736 | tf_op jit(solution)/shard_map/ppermute | solution.py:172
  3.7 24.9 %collective-permute-start.1 = (bf16[512,1024]{1,0:T(8,128)(2,1)}, bf16[512,1024]{1,0:T(8,128)(2,1)}, u32[]{:S(2)}, u32[]{:S(2)}) collective-permute-start(bf16[512,1024]{1,0:T(8,128)(2,1)} %bitcast.121), channel_id=1, source_target_pairs={{0,8},{4,12},{8,0},{12,4},{1,9},{5,13},{9,1},{13,5},{2,10},{6,14},... | collective-permute-start | bytes 3145736 | tf_op jit(solution)/shard_map/ppermute | solution.py:172
  7.9 26.0 %collective-permute-start.4 = (bf16[3,88,1024]{2,1,0:T(8,128)(2,1)S(1)}, bf16[3,88,1024]{2,1,0:T(8,128)(2,1)S(1)}, u32[]{:S(2)}, u32[]{:S(2)}) collective-permute-start(bf16[3,88,1024]{2,1,0:T(8,128)(2,1)S(1)} %dynamic-slice_bitcast_fusion.2), channel_id=1, source_target_pairs={{0,2},{1,3},{2,0},{3,1},{4,6},{5,7},{6,4},{7,5},{8,10},{9,11},{10,... | collective-permute-start | bytes 1622024 | tf_op jit(solution)/shard_map/ppermute | solution.py:172
  29.7 12.5 %collective-permute-start.2 = (bf16[256,1024]{1,0:T(8,128)(2,1)S(1)}, bf16[256,1024]{1,0:T(8,128)(2,1)S(1)}, u32[]{:S(2)}, u32[]{:S(2)}) collective-permute-start(bf16[256,1024]{1,0:T(8,128)(2,1)S(1)} %slice.165), channel_id=1, source_target_pairs={{0,4},{4,0},{8,12},{12,8},{1,5},{5,1},{9,13},{13,9},{2,6},{6,2},{1... | collective-permute-start | bytes 1572872 | tf_op jit(solution)/shard_map/ppermute | solution.py:172
  31.2 12.6 %collective-permute-start.3 = (bf16[256,1024]{1,0:T(8,128)(2,1)S(1)}, bf16[256,1024]{1,0:T(8,128)(2,1)S(1)}, u32[]{:S(2)}, u32[]{:S(2)}) collective-permute-start(bf16[256,1024]{1,0:T(8,128)(2,1)S(1)} %slice.166), channel_id=1, source_target_pairs={{0,8},{4,12},{8,0},{12,4},{1,9},{5,13},{9,1},{13,5},{2,10},{6,14},... | collective-permute-start | bytes 1572872 | tf_op jit(solution)/shard_map/ppermute | solution.py:172
  44.6 54.5 %collective-permute-start.5 = (bf16[392,1024]{1,0:T(8,128)(2,1)}, bf16[392,1024]{1,0:T(8,128)(2,1)S(1)}, u32[]{:S(2)}, u32[]{:S(2)}) collective-permute-start(bf16[392,1024]{1,0:T(8,128)(2,1)} %after.16), channel_id=1, source_target_pairs={{0,4},{4,0},{8,12},{12,8},{1,5},{5,1},{9,13},{13,9},{2,6},{6,2},{1... | collective-permute-start | bytes 2408456 | tf_op jit(solution)/shard_map/ppermute | solution.py:172
  45.9 50.4 %collective-permute-start.6 = (bf16[392,1024]{1,0:T(8,128)(2,1)}, bf16[392,1024]{1,0:T(8,128)(2,1)S(1)}, u32[]{:S(2)}, u32[]{:S(2)}) collective-permute-start(bf16[392,1024]{1,0:T(8,128)(2,1)} %after.16), channel_id=1, source_target_pairs={{0,8},{4,12},{8,0},{12,4},{1,9},{5,13},{9,1},{13,5},{2,10},{6,14},... | collective-permute-start | bytes 2408456 | tf_op jit(solution)/shard_map/ppermute | solution.py:172
  47.5 47.0 %collective-permute-start.7 = (bf16[392,1024]{1,0:T(8,128)(2,1)}, bf16[392,1024]{1,0:T(8,128)(2,1)}, u32[]{:S(2)}, u32[]{:S(2)}) collective-permute-start(bf16[392,1024]{1,0:T(8,128)(2,1)} %after.16), channel_id=1, source_target_pairs={{0,12},{4,8},{8,4},{12,0},{1,13},{5,9},{9,5},{13,1},{2,14},{6,10},... | collective-permute-start | bytes 2408456 | tf_op jit(solution)/shard_map/ppermute | solution.py:172
  104.1 6.7 %collective-permute-start.8 = (bf16[4,128,1024]{2,1,0:T(8,128)(2,1)S(1)}, bf16[4,128,1024]{2,1,0:T(8,128)(2,1)}, u32[]{:S(2)}, u32[]{:S(2)}) collective-permute-start(bf16[4,128,1024]{2,1,0:T(8,128)(2,1)S(1)} %bitcast.118), channel_id=1, source_target_pairs={{0,16},{16,0},{1,17},{17,1},{2,18},{18,2},{3,19},{19,3},{4,20},{20... | collective-permute-start | bytes 3145736 | tf_op jit(solution)/shard_map/ppermute | solution.py:172
  105.8 23.1 %collective-permute-start.9 = (bf16[1056,1024]{1,0:T(8,128)(2,1)}, bf16[1056,1024]{1,0:T(8,128)(2,1)}, u32[]{:S(2)}, u32[]{:S(2)}) collective-permute-start(bf16[1056,1024]{1,0:T(8,128)(2,1)} %bitcast.24.refs_3_.refs_4_.refs_5_.far_ref), channel_id=1, source_target_pairs={{0,16},{16,0},{1,17},{17,1},{2,18},{18,2},{3,19},{19,3},{4,20},{20... | collective-permute-start | bytes 6488072 | tf_op jit(solution)/shard_map/ppermute | solution.py:172
  106.3 17.8 %all-to-all-start = ((bf16[4,512,256]{2,1,0:T(8,128)(2,1)}), bf16[4,512,256]{2,1,0:T(8,128)(2,1)S(1)}, u32[]{:S(2)}, u32[]{:S(2)}) async-start(bf16[4,512,256]{2,1,0:T(8,128)(2,1)} %bitcast.7), calls=%async_computation | async-start | bytes 2097152 | tf_op jit(solution)/shard_map/all_to_all | solution.py:703
  110.0 36.5 %collective-permute-start.11 = (bf16[512,1024]{1,0:T(8,128)(2,1)}, bf16[512,1024]{1,0:T(8,128)(2,1)}, u32[]{:S(2)}, u32[]{:S(2)}) collective-permute-start(bf16[512,1024]{1,0:T(8,128)(2,1)} %bitcast.15.g_ref.refs_4_), channel_id=1, source_target_pairs={{0,1},{1,0},{2,3},{3,2},{4,5},{5,4},{6,7},{7,6},{8,9},{9,8},{10,11... | collective-permute-start | bytes 3145736 | tf_op jit(solution)/shard_map/ppermute | solution.py:172
  128.9 29.0 %collective-permute-start.10 = (bf16[512,1024]{1,0:T(8,128)(2,1)S(1)}, bf16[512,1024]{1,0:T(8,128)(2,1)S(1)}, u32[]{:S(2)}, u32[]{:S(2)}) collective-permute-start(bf16[512,1024]{1,0:T(8,128)(2,1)S(1)} %multiply_convert_fusion.x_ref.refs_2_), channel_id=1, source_target_pairs={{0,1},{1,0},{2,3},{3,2},{4,5},{5,4},{6,7},{7,6},{8,9},{9,8},{10,11... | collective-permute-start | bytes 3145736 | tf_op jit(solution)/shard_map/ppermute | solution.py:172
  182.5 17.5 %collective-permute-start.13 = (bf16[1056,1024]{1,0:T(8,128)(2,1)}, bf16[1056,1024]{1,0:T(8,128)(2,1)}, u32[]{:S(2)}, u32[]{:S(2)}) collective-permute-start(bf16[1056,1024]{1,0:T(8,128)(2,1)} %far_other.1), channel_id=1, source_target_pairs={{0,16},{16,0},{1,17},{17,1},{2,18},{18,2},{3,19},{19,3},{4,20},{20... | collective-permute-start | bytes 6488072 | tf_op jit(solution)/shard_map/ppermute | solution.py:172
  182.7 25.9 %collective-permute-start.12 = (bf16[512,1024]{1,0:T(8,128)(2,1)}, bf16[512,1024]{1,0:T(8,128)(2,1)}, u32[]{:S(2)}, u32[]{:S(2)}) collective-permute-start(bf16[512,1024]{1,0:T(8,128)(2,1)} %get-tuple-element.64), channel_id=1, source_target_pairs={{0,1},{1,0},{2,3},{3,2},{4,5},{5,4},{6,7},{7,6},{8,9},{9,8},{10,11... | collective-permute-start | bytes 3145736 | tf_op jit(solution)/shard_map/ppermute | solution.py:172
  211.3 37.5 %collective-permute-start.14 = (bf16[1056,1024]{1,0:T(8,128)(2,1)}, bf16[1056,1024]{1,0:T(8,128)(2,1)}, u32[]{:S(2)}, u32[]{:S(2)}) collective-permute-start(bf16[1056,1024]{1,0:T(8,128)(2,1)} %after.21), channel_id=1, source_target_pairs={{0,16},{16,0},{1,17},{17,1},{2,18},{18,2},{3,19},{19,3},{4,20},{20... | collective-permute-start | bytes 6488072 | tf_op jit(solution)/shard_map/ppermute | solution.py:172
  217.4 31.4 %collective-permute-start.18 = (bf16[4,128,1024]{2,1,0:T(8,128)(2,1)}, bf16[4,128,1024]{2,1,0:T(8,128)(2,1)}, u32[]{:S(2)}, u32[]{:S(2)}) collective-permute-start(bf16[4,128,1024]{2,1,0:T(8,128)(2,1)} %get-tuple-element.111), channel_id=1, source_target_pairs={{0,16},{16,0},{1,17},{17,1},{2,18},{18,2},{3,19},{19,3},{4,20},{20... | collective-permute-start | bytes 3145736 | tf_op jit(solution)/shard_map/ppermute | solution.py:172
  218.1 16.3 %collective-permute-start.17 = (bf16[3,88,1024]{2,1,0:T(8,128)(2,1)}, bf16[3,88,1024]{2,1,0:T(8,128)(2,1)S(1)}, u32[]{:S(2)}, u32[]{:S(2)}) collective-permute-start(bf16[3,88,1024]{2,1,0:T(8,128)(2,1)} %get-tuple-element.68), channel_id=1, source_target_pairs={{0,12},{4,8},{8,4},{12,0},{1,13},{5,9},{9,5},{13,1},{2,14},{6,10},... | collective-permute-start | bytes 1622024 | tf_op jit(solution)/shard_map/ppermute | solution.py:172
  220.7 25.4 %collective-permute-start.16 = (bf16[3,88,1024]{2,1,0:T(8,128)(2,1)}, bf16[3,88,1024]{2,1,0:T(8,128)(2,1)}, u32[]{:S(2)}, u32[]{:S(2)}) collective-permute-start(bf16[3,88,1024]{2,1,0:T(8,128)(2,1)} %get-tuple-element.67), channel_id=1, source_target_pairs={{0,8},{4,12},{8,0},{12,4},{1,9},{5,13},{9,1},{13,5},{2,10},{6,14},... | collective-permute-start | bytes 1622024 | tf_op jit(solution)/shard_map/ppermute | solution.py:172
  221.3 25.1 %collective-permute-start.15 = (bf16[3,88,1024]{2,1,0:T(8,128)(2,1)}, bf16[3,88,1024]{2,1,0:T(8,128)(2,1)}, u32[]{:S(2)}, u32[]{:S(2)}) collective-permute-start(bf16[3,88,1024]{2,1,0:T(8,128)(2,1)} %get-tuple-element.66), channel_id=1, source_target_pairs={{0,4},{4,0},{8,12},{12,8},{1,5},{5,1},{9,13},{13,9},{2,6},{6,2},{1... | collective-permute-start | bytes 1622024 | tf_op jit(solution)/shard_map/ppermute | solution.py:172
  226.3 32.0 %all-to-all-start.1 = ((bf16[4,512,256]{2,1,0:T(8,128)(2,1)}), bf16[4,512,256]{2,1,0:T(8,128)(2,1)S(1)}, u32[]{:S(2)}, u32[]{:S(2)}) async-start(bf16[4,512,256]{2,1,0:T(8,128)(2,1)} %fusion.10.refs_1_), calls=%async_computation.1 | async-start | bytes 2097152 | tf_op jit(solution)/shard_map/all_to_all | solution.py:744
  248.8 63.1 %collective-permute-start.23 = (bf16[3,88,1024]{2,1,0:T(8,128)(2,1)}, bf16[3,88,1024]{2,1,0:T(8,128)(2,1)}, u32[]{:S(2)}, u32[]{:S(2)}) collective-permute-start(bf16[3,88,1024]{2,1,0:T(8,128)(2,1)} %add_convert_fusion.3.refs_2_.rest_0_), channel_id=1, source_target_pairs={{0,2},{1,3},{2,0},{3,1},{4,6},{5,7},{6,4},{7,5},{8,10},{9,11},{10,... | collective-permute-start | bytes 1622024 | tf_op jit(solution)/shard_map/ppermute | solution.py:172
  259.3 83.1 %collective-permute-start.19 = (bf16[512,1024]{1,0:T(8,128)(2,1)}, bf16[512,1024]{1,0:T(8,128)(2,1)S(1)}, u32[]{:S(2)}, u32[]{:S(2)}) collective-permute-start(bf16[512,1024]{1,0:T(8,128)(2,1)} %after.24), channel_id=1, source_target_pairs={{0,1},{1,0},{2,3},{3,2},{4,5},{5,4},{6,7},{7,6},{8,9},{9,8},{10,11... | collective-permute-start | bytes 3145736 | tf_op jit(solution)/shard_map/ppermute | solution.py:172
  260.3 49.1 %collective-permute-start.22 = (bf16[392,1024]{1,0:T(8,128)(2,1)}, bf16[392,1024]{1,0:T(8,128)(2,1)S(1)}, u32[]{:S(2)}, u32[]{:S(2)}) collective-permute-start(bf16[392,1024]{1,0:T(8,128)(2,1)} %after.27.rest_3_), channel_id=1, source_target_pairs={{0,12},{4,8},{8,4},{12,0},{1,13},{5,9},{9,5},{13,1},{2,14},{6,10},... | collective-permute-start | bytes 2408456 | tf_op jit(solution)/shard_map/ppermute | solution.py:172
  262.0 47.4 %collective-permute-start.21 = (bf16[392,1024]{1,0:T(8,128)(2,1)S(1)}, bf16[392,1024]{1,0:T(8,128)(2,1)S(1)}, u32[]{:S(2)}, u32[]{:S(2)}) collective-permute-start(bf16[392,1024]{1,0:T(8,128)(2,1)S(1)} %copy-done.3), channel_id=1, source_target_pairs={{0,8},{4,12},{8,0},{12,4},{1,9},{5,13},{9,1},{13,5},{2,10},{6,14},... | collective-permute-start | bytes 2408456 | tf_op jit(solution)/shard_map/ppermute | solution.py:172
  263.2 46.2 %collective-permute-start.20 = (bf16[392,1024]{1,0:T(8,128)(2,1)S(1)}, bf16[392,1024]{1,0:T(8,128)(2,1)S(1)}, u32[]{:S(2)}, u32[]{:S(2)}) collective-permute-start(bf16[392,1024]{1,0:T(8,128)(2,1)S(1)} %copy-done.4), channel_id=1, source_target_pairs={{0,4},{4,0},{8,12},{12,8},{1,5},{5,1},{9,13},{13,9},{2,6},{6,2},{1... | collective-permute-start | bytes 2408456 | tf_op jit(solution)/shard_map/ppermute | solution.py:172
  314.2 29.9 %collective-permute-start.50 = (bf16[3,88,1024]{2,1,0:T(8,128)(2,1)}, bf16[3,88,1024]{2,1,0:T(8,128)(2,1)S(1)}, u32[]{:S(2)}, u32[]{:S(2)}) collective-permute-start(bf16[3,88,1024]{2,1,0:T(8,128)(2,1)} %get-tuple-element.92.refs_14_), channel_id=1, source_target_pairs={{0,4},{4,0},{8,12},{12,8},{1,5},{5,1},{9,13},{13,9},{2,6},{6,2},{1... | collective-permute-start | bytes 1622024 | tf_op jit(solution)/shard_map/ppermute | solution.py:172
  315.7 29.3 %collective-permute-start.51 = (bf16[3,88,1024]{2,1,0:T(8,128)(2,1)}, bf16[3,88,1024]{2,1,0:T(8,128)(2,1)S(1)}, u32[]{:S(2)}, u32[]{:S(2)}) collective-permute-start(bf16[3,88,1024]{2,1,0:T(8,128)(2,1)} %get-tuple-element.92.refs_14_), channel_id=1, source_target_pairs={{0,8},{4,12},{8,0},{12,4},{1,9},{5,13},{9,1},{13,5},{2,10},{6,14},... | collective-permute-start | bytes 1622024 | tf_op jit(solution)/shard_map/ppermute | solution.py:172
  316.4 28.8 %collective-permute-start.52 = (bf16[3,88,1024]{2,1,0:T(8,128)(2,1)}, bf16[3,88,1024]{2,1,0:T(8,128)(2,1)}, u32[]{:S(2)}, u32[]{:S(2)}) collective-permute-start(bf16[3,88,1024]{2,1,0:T(8,128)(2,1)} %get-tuple-element.92.refs_14_), channel_id=1, source_target_pairs={{0,12},{4,8},{8,4},{12,0},{1,13},{5,9},{9,5},{13,1},{2,14},{6,10},... | collective-permute-start | bytes 1622024 | tf_op jit(solution)/shard_map/ppermute | solution.py:172
  334.6 13.2 %collective-permute-start.24 = (bf16[256,1024]{1,0:T(8,128)(2,1)S(1)}, bf16[256,1024]{1,0:T(8,128)(2,1)S(1)}, u32[]{:S(2)}, u32[]{:S(2)}) collective-permute-start(bf16[256,1024]{1,0:T(8,128)(2,1)S(1)} %get-tuple-element.105), channel_id=1, source_target_pairs={{0,8},{4,12},{8,0},{12,4},{1,9},{5,13},{9,1},{13,5},{2,10},{6,14},... | collective-permute-start | bytes 1572872 | tf_op jit(solution)/shard_map/ppermute | solution.py:172
  344.1 14.6 %collective-permute-start.27 = (bf16[256,1024]{1,0:T(8,128)(2,1)}, bf16[256,1024]{1,0:T(8,128)(2,1)}, u32[]{:S(2)}, u32[]{:S(2)}) collective-permute-start(bf16[256,1024]{1,0:T(8,128)(2,1)} %get-tuple-element.104), channel_id=1, source_target_pairs={{0,4},{4,0},{8,12},{12,8},{1,5},{5,1},{9,13},{13,9},{2,6},{6,2},{1... | collective-permute-start | bytes 1572872 | tf_op jit(solution)/shard_map/ppermute | solution.py:172
  346.3 89.8 %collective-permute-start.53 = (bf16[3,352,1024]{2,1,0:T(8,128)(2,1)S(1)}, bf16[3,352,1024]{2,1,0:T(8,128)(2,1)}, u32[]{:S(2)}, u32[]{:S(2)}) collective-permute-start(bf16[3,352,1024]{2,1,0:T(8,128)(2,1)S(1)} %bitcast.115), channel_id=1, source_target_pairs={{0,16},{16,0},{1,17},{17,1},{2,18},{18,2},{3,19},{19,3},{4,20},{20... | collective-permute-start | bytes 6488072 | tf_op jit(solution)/shard_map/ppermute | solution.py:172
  347.7 12.9 %collective-permute-start.31 = (bf16[128,768]{1,0:T(8,128)(2,1)}, bf16[128,768]{1,0:T(8,128)(2,1)}, u32[]{:S(2)}, u32[]{:S(2)}) collective-permute-start(bf16[128,768]{1,0:T(8,128)(2,1)} %get-tuple-element.118), channel_id=1, source_target_pairs={{0,3},{1,2},{2,1},{3,0},{4,7},{5,6},{6,5},{7,4},{8,11},{9,10},{10,... | collective-permute-start | bytes 589832 | tf_op jit(solution)/shard_map/ppermute | solution.py:172
  347.7 16.8 %collective-permute-start.30 = (bf16[128,768]{1,0:T(8,128)(2,1)}, bf16[128,768]{1,0:T(8,128)(2,1)}, u32[]{:S(2)}, u32[]{:S(2)}) collective-permute-start(bf16[128,768]{1,0:T(8,128)(2,1)} %get-tuple-element.119), channel_id=1, source_target_pairs={{0,2},{1,3},{2,0},{3,1},{4,6},{5,7},{6,4},{7,5},{8,10},{9,11},{10,... | collective-permute-start | bytes 589832 | tf_op jit(solution)/shard_map/ppermute | solution.py:172
  347.7 16.8 %collective-permute-start.29 = (bf16[128,768]{1,0:T(8,128)(2,1)}, bf16[128,768]{1,0:T(8,128)(2,1)}, u32[]{:S(2)}, u32[]{:S(2)}) collective-permute-start(bf16[128,768]{1,0:T(8,128)(2,1)} %get-tuple-element.117), channel_id=1, source_target_pairs={{0,1},{1,0},{2,3},{3,2},{4,5},{5,4},{6,7},{7,6},{8,9},{9,8},{10,11... | collective-permute-start | bytes 589832 | tf_op jit(solution)/shard_map/ppermute | solution.py:172
  366.6 10.0 %collective-permute-start.32 = (bf16[128,768]{1,0:T(8,128)(2,1)}, bf16[128,768]{1,0:T(8,128)(2,1)}, u32[]{:S(2)}, u32[]{:S(2)}) collective-permute-start(bf16[128,768]{1,0:T(8,128)(2,1)} %get-tuple-element.96), channel_id=1, source_target_pairs={{0,3},{1,2},{2,1},{3,0},{4,7},{5,6},{6,5},{7,4},{8,11},{9,10},{10,... | collective-permute-start | bytes 589832 | tf_op jit(solution)/shard_map/ppermute | solution.py:172
  368.8 59.3 %collective-permute-start.28 = (bf16[512,1024]{1,0:T(8,128)(2,1)}, bf16[512,1024]{1,0:T(8,128)(2,1)}, u32[]{:S(2)}, u32[]{:S(2)}) collective-permute-start(bf16[512,1024]{1,0:T(8,128)(2,1)} %pad_maximum_fusion.6), channel_id=1, source_target_pairs={{0,8},{4,12},{8,0},{12,4},{1,9},{5,13},{9,1},{13,5},{2,10},{6,14},... | collective-permute-start | bytes 3145736 | tf_op jit(solution)/shard_map/ppermute | solution.py:172
  370.1 11.4 %collective-permute-start.40 = (bf16[128,768]{1,0:T(8,128)(2,1)}, bf16[128,768]{1,0:T(8,128)(2,1)}, u32[]{:S(2)}, u32[]{:S(2)}) collective-permute-start(bf16[128,768]{1,0:T(8,128)(2,1)} %get-tuple-element.96), channel_id=1, source_target_pairs={{0,1},{1,0},{2,3},{3,2},{4,5},{5,4},{6,7},{7,6},{8,9},{9,8},{10,11... | collective-permute-start | bytes 589832 | tf_op jit(solution)/shard_map/ppermute | solution.py:172
  372.0 13.5 %collective-permute-start.41 = (bf16[128,768]{1,0:T(8,128)(2,1)}, bf16[128,768]{1,0:T(8,128)(2,1)S(1)}, u32[]{:S(2)}, u32[]{:S(2)}) collective-permute-start(bf16[128,768]{1,0:T(8,128)(2,1)} %get-tuple-element.96), channel_id=1, source_target_pairs={{0,2},{1,3},{2,0},{3,1},{4,6},{5,7},{6,4},{7,5},{8,10},{9,11},{10,... | collective-permute-start | bytes 589832 | tf_op jit(solution)/shard_map/ppermute | solution.py:172
  376.5 9.0 %collective-permute-start.33 = (f32[3,1024]{1,0:T(4,128)}, f32[3,1024]{1,0:T(4,128)S(1)}, u32[]{:S(2)}, u32[]{:S(2)}) collective-permute-start(f32[3,1024]{1,0:T(4,128)} %after.30), channel_id=1, source_target_pairs={{0,16},{16,0},{1,17},{17,1},{2,18},{18,2},{3,19},{19,3},{4,20},{20... | collective-permute-start | bytes 36872 | tf_op jit(solution)/shard_map/ppermute | solution.py:172
  386.3 8.3 %collective-permute-start.35 = (f32[3,1024]{1,0:T(4,128)S(1)}, f32[3,1024]{1,0:T(4,128)S(1)}, u32[]{:S(2)}, u32[]{:S(2)}) collective-permute-start(f32[3,1024]{1,0:T(4,128)S(1)} %add.274), channel_id=1, source_target_pairs={{0,8},{4,12},{8,0},{12,4},{1,9},{5,13},{9,1},{13,5},{2,10},{6,14},... | collective-permute-start | bytes 36872 | tf_op jit(solution)/shard_map/ppermute | solution.py:172
  387.6 9.0 %collective-permute-start.36 = (f32[3,1024]{1,0:T(4,128)S(1)}, f32[3,1024]{1,0:T(4,128)S(1)}, u32[]{:S(2)}, u32[]{:S(2)}) collective-permute-start(f32[3,1024]{1,0:T(4,128)S(1)} %add.274), channel_id=1, source_target_pairs={{0,12},{4,8},{8,4},{12,0},{1,13},{5,9},{9,5},{13,1},{2,14},{6,10},... | collective-permute-start | bytes 36872 | tf_op jit(solution)/shard_map/ppermute | solution.py:172
  389.1 7.6 %collective-permute-start.34 = (f32[3,1024]{1,0:T(4,128)S(1)}, f32[3,1024]{1,0:T(4,128)S(1)}, u32[]{:S(2)}, u32[]{:S(2)}) collective-permute-start(f32[3,1024]{1,0:T(4,128)S(1)} %add.274), channel_id=1, source_target_pairs={{0,4},{4,0},{8,12},{12,8},{1,5},{5,1},{9,13},{13,9},{2,6},{6,2},{1... | collective-permute-start | bytes 36872 | tf_op jit(solution)/shard_map/ppermute | solution.py:172
  394.5 6.4 %collective-permute-start.45 = (bf16[32,1024]{1,0:T(8,128)(2,1)S(1)}, bf16[32,1024]{1,0:T(8,128)(2,1)S(1)}, u32[]{:S(2)}, u32[]{:S(2)}) collective-permute-start(bf16[32,1024]{1,0:T(8,128)(2,1)S(1)} %get-tuple-element.123), channel_id=1, source_target_pairs={{0,3},{1,2},{2,1},{3,0},{4,7},{5,6},{6,5},{7,4},{8,11},{9,10},{10,... | collective-permute-start | bytes 196616 | tf_op jit(solution)/shard_map/ppermute | solution.py:172
  396.7 6.7 %collective-permute-start.44 = (bf16[32,1024]{1,0:T(8,128)(2,1)S(1)}, bf16[32,1024]{1,0:T(8,128)(2,1)S(1)}, u32[]{:S(2)}, u32[]{:S(2)}) collective-permute-start(bf16[32,1024]{1,0:T(8,128)(2,1)S(1)} %get-tuple-element.124), channel_id=1, source_target_pairs={{0,2},{1,3},{2,0},{3,1},{4,6},{5,7},{6,4},{7,5},{8,10},{9,11},{10,... | collective-permute-start | bytes 196616 | tf_op jit(solution)/shard_map/ppermute | solution.py:172
  396.7 8.4 %collective-permute-start.43 = (bf16[32,1024]{1,0:T(8,128)(2,1)S(1)}, bf16[32,1024]{1,0:T(8,128)(2,1)S(1)}, u32[]{:S(2)}, u32[]{:S(2)}) collective-permute-start(bf16[32,1024]{1,0:T(8,128)(2,1)S(1)} %get-tuple-element.122), channel_id=1, source_target_pairs={{0,1},{1,0},{2,3},{3,2},{4,5},{5,4},{6,7},{7,6},{8,9},{9,8},{10,11... | collective-permute-start | bytes 196616 | tf_op jit(solution)/shard_map/ppermute | solution.py:172
  406.0 22.7 %collective-permute-start.26 = (bf16[512,1024]{1,0:T(8,128)(2,1)}, bf16[512,1024]{1,0:T(8,128)(2,1)S(1)}, u32[]{:S(2)}, u32[]{:S(2)}) collective-permute-start(bf16[512,1024]{1,0:T(8,128)(2,1)} %pad_maximum_fusion.5), channel_id=1, source_target_pairs={{0,4},{4,0},{8,12},{12,8},{1,5},{5,1},{9,13},{13,9},{2,6},{6,2},{1... | collective-permute-start | bytes 3145736 | tf_op jit(solution)/shard_map/ppermute | solution.py:172
  409.0 25.1 %collective-permute-start.42 = (bf16[512,768]{1,0:T(8,128)(2,1)S(1)}, bf16[512,768]{1,0:T(8,128)(2,1)S(1)}, u32[]{:S(2)}, u32[]{:S(2)}) collective-permute-start(bf16[512,768]{1,0:T(8,128)(2,1)S(1)} %constant_dynamic-update-slice_fusion.7), channel_id=1, source_target_pairs={{0,16},{16,0},{1,17},{17,1},{2,18},{18,2},{3,19},{19,3},{4,20},{20... | collective-permute-start | bytes 2359304 | tf_op jit(solution)/shard_map/ppermute | solution.py:172
  (61 other events, 585.3 us)
